TPU v7x, 512 devices: a whole 4x4x16 slice. The times are simulated.
512 devices in a mesh: expert: 2 (over x_hi), dp: 16 (over z), seq: 16 (over y, x_lo, core).
Axes of the slice: x: 4 (x_hi: 2, x_lo: 2; x = x_hi * 2 + x_lo), y: 4, z: 16, core: 2. Of those that a mesh axis runs over, the one named last changes fastest.
Arguments:
- queries: bfloat16 [32, 2048, 4096], P(('expert', 'dp'), 'seq'), may hold values from -6 to 6
- key_states: bfloat16 [32, 2048, 4096], P(('expert', 'dp'), 'seq'), may hold values from -6 to 6
- value_states: bfloat16 [32, 2048, 4096], P(('expert', 'dp'), 'seq'), may hold values from -6 to 6
- timesteps: int32 [32], P(('expert', 'dp')), may hold values from 0 to 999, as said below
- norm_gain: bfloat16 [2, 2, 4096], P('expert'), may hold values from 0.3984375 to 2.5
- cross_gain: bfloat16 [2, 4096], P('expert', 'seq'), may hold values from 0.3984375 to 2.5
- prompt_states: bfloat16 [2, 2, 2, 128, 4096], P('expert', None, None, None, 'seq'), may hold values from -52 to 52
- prompt_lengths: int32 [2], replicated, may hold values from 16 to 128, as said below
Outputs:
- guided: bfloat16 [32, 2048, 4096], P(('expert', 'dp'), 'seq')
Inputs may be any that keep to these rules, and one draw needn't show every extreme that they name: `timesteps`: sample 0 has a timestep of at least 875, sample 1 one below it. `prompt_lengths`: one of the two equals 128.
All inputs are finite; a program needn't handle non-finite values.
Results may differ from a plain program's by a relative error of at most 0.035.
Values may be sent and summed in bfloat16 or wider, within the bound.
A program may use at most 128 MiB of HBM per device.

v0:
```python
import math

import jax
import jax.numpy as jnp
from jax import lax
from jax.sharding import PartitionSpec as P

HEAD_DIM = 128
BOUNDARY = 875


GUIDANCE = 5.0


def swapped(value, axis, stride):
    mask = 2**stride
    pairs = [(source, source ^ mask) for source in range(lax.axis_size(axis))]
    return lax.ppermute(value, axis, pairs)


def rms_scale(values, gain):
    mean_square = jnp.mean(values * values, axis=-1, keepdims=True)
    return values * lax.rsqrt(mean_square + 1e-06) * gain.astype(jnp.float32)


def attend_block(query_rows, key_rows, value_rows, visible):
    scores = jnp.einsum(
        "rhd,khd->hrk", query_rows, key_rows, preferred_element_type=jnp.float32
    ) * HEAD_DIM ** (-0.5)
    if visible is not None:
        scores = jnp.where(visible, scores, -jnp.inf)
    row_peak = jnp.max(scores, axis=-1, keepdims=True)
    weights = jnp.exp(scores - row_peak)
    probabilities = (weights / jnp.sum(weights, axis=-1, keepdims=True)).astype(jnp.bfloat16)
    return jnp.einsum("hrk,khd->rhd", probabilities, value_rows, preferred_element_type=jnp.float32)


def teacher_slots(query_in, key_in, value_in, gains, cross_scale, tables, prompt_lengths):
    slot_count, tok_rows, feature_width = query_in.shape
    seq_parts = lax.axis_size("seq")
    head_cols = feature_width // seq_parts
    local_heads = head_cols // HEAD_DIM
    query_normed = rms_scale(query_in.astype(jnp.float32), gains[:, 0, None, :]).astype(
        jnp.bfloat16
    )
    key_normed = rms_scale(key_in.astype(jnp.float32), gains[:, 1, None, :]).astype(jnp.bfloat16)
    packed = jnp.stack([query_normed, key_normed, value_in], axis=1).reshape(
        slot_count, 3, tok_rows, seq_parts, head_cols
    )
    spread = lax.all_to_all(packed, "seq", split_axis=3, concat_axis=2, tiled=True)
    length = tok_rows * seq_parts
    spread = spread.reshape(slot_count, 3, length, local_heads, HEAD_DIM)
    block_rows = math.gcd(length, 512)
    prompt_heads = tables.reshape(slot_count, 2, 2, tables.shape[3], local_heads, HEAD_DIM)
    visible = jnp.arange(tables.shape[3])[None, :] < prompt_lengths[:, None]
    cross_heads = cross_scale.reshape(slot_count, local_heads, HEAD_DIM)
    row_starts = jnp.arange(length // block_rows, dtype=jnp.int32) * block_rows

    def one_block(row_start):
        query_rows = lax.dynamic_slice_in_dim(spread[0, 0], row_start, block_rows, 0)
        self_out = attend_block(query_rows, spread[0, 1], spread[0, 2], None).astype(jnp.bfloat16)
        cross_query = rms_scale(self_out.astype(jnp.float32), cross_heads[0]).astype(jnp.bfloat16)
        positive = attend_block(
            cross_query, prompt_heads[0, 0, 0], prompt_heads[0, 0, 1], visible[0][None, None, :]
        )
        negative = attend_block(
            cross_query, prompt_heads[0, 1, 0], prompt_heads[0, 1, 1], visible[1][None, None, :]
        )
        return (self_out.astype(jnp.float32) + negative + GUIDANCE * (positive - negative)).astype(
            jnp.bfloat16
        )

    outputs = [lax.map(one_block, row_starts).reshape(length, head_cols)]
    merged = jnp.stack(outputs).reshape(slot_count, seq_parts, tok_rows, head_cols)
    returned = lax.all_to_all(merged, "seq", split_axis=1, concat_axis=3, tiled=True)
    return returned.reshape(slot_count, tok_rows, feature_width)


def body(
    queries,
    key_states,
    value_states,
    timesteps,
    norm_gain,
    cross_gain,
    prompt_states,
    prompt_lengths,
):
    own_group = lax.axis_index("expert")
    routed_group = jnp.where(timesteps[0] >= BOUNDARY, 0, 1).astype(jnp.int32)
    remote = swapped((norm_gain[0], cross_gain[0], prompt_states[0]), "expert", 0)
    chosen = routed_group == own_group
    gains = jnp.where(chosen, norm_gain[0], remote[0])
    cross_scale = jnp.where(chosen, cross_gain[0], remote[1])
    tables = jnp.where(chosen, prompt_states[0], remote[2])
    output = teacher_slots(
        queries,
        key_states,
        value_states,
        gains[None],
        cross_scale[None],
        tables[None],
        prompt_lengths,
    )[0]
    return output[None]


def solution(mesh):
    placed = (
        P(("expert", "dp"), "seq", None),
        P(("expert", "dp"), "seq", None),
        P(("expert", "dp"), "seq", None),
        P(("expert", "dp")),
        P("expert", None, None),
        P("expert", "seq"),
        P("expert", None, None, None, "seq"),
        P(),
    )
    return jax.shard_map(
        body,
        mesh=mesh,
        in_specs=placed,
        out_specs=P(("expert", "dp"), "seq", None),
        check_vma=False,
    )
```

profile of v0, /device:TPU:1, one launch (start us, length us, event | category | flops | bytes accessed | tf_op | source)
XLA Modules:
  0.0 243.0 jit_solution(2992826222816055362)
XLA Ops:
  0.0 5.6 %collective-permute-start = (bf16[2,4096]{1,0:T(2,128)(2,1)}, bf16[2,4096]{1,0:T(2,128)(2,1)S(1)}, u32[]{:S(2)}, u32[]{:S(2)}) collective-permute-start(bf16[2,4096]{1,0:T(2,128)(2,1)} %bitcast.123), channel_id=1, source_target_pairs={{0,256},{256,0},{1,257},{257,1},{2,258},{258,2},{3,259},{259,3},{4... | collective-permute-start | bytes 49160 | tf_op jit(solution)/shard_map/ppermute | solution.py:18
  5.6 1.5 fusion.48
  7.1 1.5 fusion.51
  9.3 2.4 copy.55
  12.1 1.3 copy.53
  14.7 3.2 %pad_maximum_fusion = bf16[1,3,128,16,256]{2,4,1,0,3:T(8,128)(2,1)} fusion(bf16[1,1,128,16,256]{2,4,1,0,3:T(8,128)(2,1)S(1)} %bitcast.116, bf16[1,1,128,16,256]{2,4,1,0,3:T(8,128)(2,1)S(1)} %bitcast.118, bf16[1,1,128,16,256]{2,4,1,0,3:T(8,128)(2,1)} %bitcast.117), kind=kLoop, calls=%fused_computation.58 | loop fusion | flops 3145728 | bytes 6291456 | tf_op jit(solution)/shard_map/stack | solution.py:47
  17.9 7.0 %all-to-all-start = ((bf16[1,3,128,16,256]{2,4,1,0,3:T(8,128)(2,1)}), bf16[1,3,128,16,256]{2,4,1,0,3:T(8,128)(2,1)S(1)}, u32[]{:S(2)}, u32[]{:S(2)}) async-start(bf16[1,3,128,16,256]{2,4,1,0,3:T(8,128)(2,1)} %pad_maximum_fusion), calls=%async_computation | async-start | bytes 6291456 | tf_op jit(solution)/shard_map/all_to_all | solution.py:50
  24.9 1.1 copy.57
  26.0 5.1 %collective-permute-start.2 = (bf16[2,2,128,256]{2,3,1,0:T(8,128)(2,1)S(1)}, bf16[2,2,128,256]{2,3,1,0:T(8,128)(2,1)}, u32[]{:S(2)}, u32[]{:S(2)}) collective-permute-start(bf16[2,2,128,256]{2,3,1,0:T(8,128)(2,1)S(1)} %bitcast.119), channel_id=1, source_target_pairs={{0,256},{256,0},{1,257},{257,1},{2,258},{258,2},{3,259},{259,3},{4... | collective-permute-start | bytes 786440 | tf_op jit(solution)/shard_map/ppermute | solution.py:18
  31.2 2.1 collective-permute-start.1
  33.4 36.7 %collective-permute-done.1 = bf16[256]{0:T(256)(128)(2,1)S(1)} collective-permute-done((bf16[256]{0:T(256)(128)(2,1)S(1)}, bf16[256]{0:T(256)(128)(2,1)S(1)}, u32[]{:S(2)}, u32[]{:S(2)}) %collective-permute-start.1) | collective-permute-done | bytes 544 | tf_op jit(solution)/shard_map/ppermute | solution.py:18
  70.8 1.8 copy.59
  72.6 3.7 %copy.56 = bf16[1,3,16,128,1,256]{3,2,5,1,4,0:T(8,128)(2,1)} copy(bf16[1,3,16,128,1,256]{3,5,1,2,4,0:T(8,128)(2,1)S(1)} %bitcast.113) | data formatting | bytes 6291456 | tf_op jit(solution)/shard_map/all_to_all | solution.py:50
  76.3 5.8 %reshape.74 = bf16[1,3,2048,2,128]{2,4,3,1,0:T(8,128)(2,1)} reshape(bf16[1,3,16,128,1,256]{3,2,5,1,4,0:T(8,128)(2,1)} %copy.56) | data formatting | bytes 6291456 | tf_op jit(solution)/shard_map/reshape | solution.py:52
  82.1 3.5 %copy.58 = bf16[1,3,2048,2,128]{4,2,3,1,0:T(8,128)(2,1)S(1)} copy(bf16[1,3,2048,2,128]{2,4,3,1,0:T(8,128)(2,1)} %reshape.74) | data formatting | bytes 6291456 | tf_op jit(solution)/shard_map/while | solution.py:73
  85.6 133.5 %while.10 = (s32[]{:T(128)}, bf16[4,512,2,128]{3,2,1,0:T(2,128)(2,1)}, bf16[1,3,2048,2,128]{4,2,3,1,0:T(8,128)(2,1)S(1)}, s32[4]{0:T(128)S(1)}, pred[2,128]{1,0:...) while((s32[]{:T(128)}, ...), condition=%wide.region_10.11_spmd, body=%wide.region_2.10_spmd.sunk | while | flops 1230643968 | bytes 91014128 | solution.py:73
  88.5 1.3 fusion.93
  89.7 3.2 %copy-done = f32[2,512,2048]{2,1,0:T(8,128)} copy-done((f32[2,512,2048]{2,1,0:T(8,128)}, f32[2,512,2048]{2,1,0:T(8,128)S(1)}, u32[]{:S(2)}) %copy-start) | copy-done | bytes 8388632 | tf_op jit(solution)/shard_map/while
  92.9 2.1 fusion.94
  95.0 2.9 %copy.74 = bf16[1,3,2048,2,128]{2,4,3,1,0:T(8,128)(2,1)} copy(bf16[1,3,2048,2,128]{4,2,3,1,0:T(8,128)(2,1)S(1)} %get-tuple-element.157) | data formatting | bytes 6291456 | tf_op jit(solution)/shard_map
  98.0 9.5 %multiply_reduce_fusion.3 = (f32[512,2]{0,1:T(2,128)S(1)}, f32[512,2,128]{0,2,1:T(8,128)}) fusion(bf16[1,3,2048,2,128]{2,4,3,1,0:T(8,128)(2,1)} %copy.74, f32[2,512]{1,0:T(2,128)S(1)} %fusion.94, f32[2,512,2048]{2,1,0:T(8,128)} %copy-done), kind=kOutput, calls=%fused_computation.34.clone.1 | convolution fusion | flops 547883008 | bytes 18358272 | tf_op jit(solution)/shard_map/while/body/eval_jaxpr/hrk,khd->rhd/dot_general | solution.py:35
  107.5 1.4 fusion.97
  109.8 1.4 fusion.95
  111.2 0.8 copy-done.2
  112.1 2.3 convolution_bitcast_fusion.3
  114.4 2.6 %fusion.99 = bf16[1,512,2,128]{1,3,2,0:T(8,128)(2,1)} fusion(f32[512,2,128]{0,2,1:T(8,128)} %convolution_bitcast_fusion.3, f32[512,2,128]{0,2,1:T(8,128)} %get-tuple-element.132, f32[2,512]{1,0:T(2,128)S(1)} %fusion.98, bf16[1,2,2,128,2,128]{5,3,4,2,1,0:T(8,128)(2,1)} %get-tuple-element.161, f32[2,512,128]{1,2,0:T(8,128)} %copy-done.1), kind=kOutput, calls=%fused_computation.26.clone.1 | convolution fusion | flops 34604160 | bytes 2428928 | tf_op jit(solution)/shard_map/while/body/eval_jaxpr/hrk,khd->rhd/dot_general | solution.py:35
  117.0 1.1 copy.75
  118.1 0.9 constant_dynamic-update-slice_fusion.2
  121.8 1.3 fusion.93
  123.1 3.2 %copy-done = f32[2,512,2048]{2,1,0:T(8,128)} copy-done((f32[2,512,2048]{2,1,0:T(8,128)}, f32[2,512,2048]{2,1,0:T(8,128)S(1)}, u32[]{:S(2)}) %copy-start) | copy-done | bytes 8388632 | tf_op jit(solution)/shard_map/while
  126.3 2.1 fusion.94
  128.4 2.9 %copy.74 = bf16[1,3,2048,2,128]{2,4,3,1,0:T(8,128)(2,1)} copy(bf16[1,3,2048,2,128]{4,2,3,1,0:T(8,128)(2,1)S(1)} %get-tuple-element.157) | data formatting | bytes 6291456 | tf_op jit(solution)/shard_map
  131.3 9.5 %multiply_reduce_fusion.3 = (f32[512,2]{0,1:T(2,128)S(1)}, f32[512,2,128]{0,2,1:T(8,128)}) fusion(bf16[1,3,2048,2,128]{2,4,3,1,0:T(8,128)(2,1)} %copy.74, f32[2,512]{1,0:T(2,128)S(1)} %fusion.94, f32[2,512,2048]{2,1,0:T(8,128)} %copy-done), kind=kOutput, calls=%fused_computation.34.clone.1 | convolution fusion | flops 547883008 | bytes 18358272 | tf_op jit(solution)/shard_map/while/body/eval_jaxpr/hrk,khd->rhd/dot_general | solution.py:35
  140.8 1.4 fusion.97
  143.1 1.4 fusion.95
  145.5 2.3 convolution_bitcast_fusion.3
  147.8 2.6 %fusion.99 = bf16[1,512,2,128]{1,3,2,0:T(8,128)(2,1)} fusion(f32[512,2,128]{0,2,1:T(8,128)} %convolution_bitcast_fusion.3, f32[512,2,128]{0,2,1:T(8,128)} %get-tuple-element.132, f32[2,512]{1,0:T(2,128)S(1)} %fusion.98, bf16[1,2,2,128,2,128]{5,3,4,2,1,0:T(8,128)(2,1)} %get-tuple-element.161, f32[2,512,128]{1,2,0:T(8,128)} %copy-done.1), kind=kOutput, calls=%fused_computation.26.clone.1 | convolution fusion | flops 34604160 | bytes 2428928 | tf_op jit(solution)/shard_map/while/body/eval_jaxpr/hrk,khd->rhd/dot_general | solution.py:35
  150.4 1.1 copy.75
  151.5 0.9 constant_dynamic-update-slice_fusion.2
  155.2 1.3 fusion.93
  156.4 3.2 %copy-done = f32[2,512,2048]{2,1,0:T(8,128)} copy-done((f32[2,512,2048]{2,1,0:T(8,128)}, f32[2,512,2048]{2,1,0:T(8,128)S(1)}, u32[]{:S(2)}) %copy-start) | copy-done | bytes 8388632 | tf_op jit(solution)/shard_map/while
  159.7 2.1 fusion.94
  161.8 2.9 %copy.74 = bf16[1,3,2048,2,128]{2,4,3,1,0:T(8,128)(2,1)} copy(bf16[1,3,2048,2,128]{4,2,3,1,0:T(8,128)(2,1)S(1)} %get-tuple-element.157) | data formatting | bytes 6291456 | tf_op jit(solution)/shard_map
  164.7 9.5 %multiply_reduce_fusion.3 = (f32[512,2]{0,1:T(2,128)S(1)}, f32[512,2,128]{0,2,1:T(8,128)}) fusion(bf16[1,3,2048,2,128]{2,4,3,1,0:T(8,128)(2,1)} %copy.74, f32[2,512]{1,0:T(2,128)S(1)} %fusion.94, f32[2,512,2048]{2,1,0:T(8,128)} %copy-done), kind=kOutput, calls=%fused_computation.34.clone.1 | convolution fusion | flops 547883008 | bytes 18358272 | tf_op jit(solution)/shard_map/while/body/eval_jaxpr/hrk,khd->rhd/dot_general | solution.py:35
  174.2 1.4 fusion.97
  176.5 1.4 fusion.95
  178.8 2.3 convolution_bitcast_fusion.3
  181.2 2.6 %fusion.99 = bf16[1,512,2,128]{1,3,2,0:T(8,128)(2,1)} fusion(f32[512,2,128]{0,2,1:T(8,128)} %convolution_bitcast_fusion.3, f32[512,2,128]{0,2,1:T(8,128)} %get-tuple-element.132, f32[2,512]{1,0:T(2,128)S(1)} %fusion.98, bf16[1,2,2,128,2,128]{5,3,4,2,1,0:T(8,128)(2,1)} %get-tuple-element.161, f32[2,512,128]{1,2,0:T(8,128)} %copy-done.1), kind=kOutput, calls=%fused_computation.26.clone.1 | convolution fusion | flops 34604160 | bytes 2428928 | tf_op jit(solution)/shard_map/while/body/eval_jaxpr/hrk,khd->rhd/dot_general | solution.py:35
  183.7 1.1 copy.75
  184.8 0.9 constant_dynamic-update-slice_fusion.2
  188.5 1.3 fusion.93
  189.8 3.2 %copy-done = f32[2,512,2048]{2,1,0:T(8,128)} copy-done((f32[2,512,2048]{2,1,0:T(8,128)}, f32[2,512,2048]{2,1,0:T(8,128)S(1)}, u32[]{:S(2)}) %copy-start) | copy-done | bytes 8388632 | tf_op jit(solution)/shard_map/while
  193.0 2.1 fusion.94
  195.1 2.9 %copy.74 = bf16[1,3,2048,2,128]{2,4,3,1,0:T(8,128)(2,1)} copy(bf16[1,3,2048,2,128]{4,2,3,1,0:T(8,128)(2,1)S(1)} %get-tuple-element.157) | data formatting | bytes 6291456 | tf_op jit(solution)/shard_map
  198.1 9.5 %multiply_reduce_fusion.3 = (f32[512,2]{0,1:T(2,128)S(1)}, f32[512,2,128]{0,2,1:T(8,128)}) fusion(bf16[1,3,2048,2,128]{2,4,3,1,0:T(8,128)(2,1)} %copy.74, f32[2,512]{1,0:T(2,128)S(1)} %fusion.94, f32[2,512,2048]{2,1,0:T(8,128)} %copy-done), kind=kOutput, calls=%fused_computation.34.clone.1 | convolution fusion | flops 547883008 | bytes 18358272 | tf_op jit(solution)/shard_map/while/body/eval_jaxpr/hrk,khd->rhd/dot_general | solution.py:35
  207.6 1.4 fusion.97
  209.9 1.4 fusion.95
  212.2 2.3 convolution_bitcast_fusion.3
  214.5 2.6 %fusion.99 = bf16[1,512,2,128]{1,3,2,0:T(8,128)(2,1)} fusion(f32[512,2,128]{0,2,1:T(8,128)} %convolution_bitcast_fusion.3, f32[512,2,128]{0,2,1:T(8,128)} %get-tuple-element.132, f32[2,512]{1,0:T(2,128)S(1)} %fusion.98, bf16[1,2,2,128,2,128]{5,3,4,2,1,0:T(8,128)(2,1)} %get-tuple-element.161, f32[2,512,128]{1,2,0:T(8,128)} %copy-done.1), kind=kOutput, calls=%fused_computation.26.clone.1 | convolution fusion | flops 34604160 | bytes 2428928 | tf_op jit(solution)/shard_map/while/body/eval_jaxpr/hrk,khd->rhd/dot_general | solution.py:35
  217.1 1.1 copy.75
  218.2 0.9 constant_dynamic-update-slice_fusion.2
  219.1 1.7 reshape_stack_reshape.3
  220.8 20.2 %all_to_all.30 = bf16[1,16,128,256]{3,2,0,1:T(8,128)(2,1)S(1)} all-to-all(bf16[1,16,128,256]{3,2,0,1:T(8,128)(2,1)S(1)} %bitcast.114), channel_id=1, replica_groups=mesh['expert'=2,'dp'=16,'seq'=16] {'seq'}, dimensions={1} | all-to-all | bytes 2097152 | tf_op jit(solution)/shard_map/all_to_all | solution.py:75
  241.7 1.3 copy.63
  (76 shorter events, 12.9 us)
Async XLA Ops:
  0.0 11.7 %copy-start.6 = (bf16[1,2,4096]{2,1,0:T(2,128)(2,1)S(1)}, bf16[1,2,4096]{2,1,0:T(2,128)(2,1)}, u32[]{:S(2)}) copy-start(bf16[1,2,4096]{2,1,0:T(2,128)(2,1)} %param.14) | copy-start | bytes 49156
  0.0 11.8 %copy-start.3 = (bf16[1,128,4096]{2,1,0:T(8,128)(2,1)S(1)}, bf16[1,128,4096]{2,1,0:T(8,128)(2,1)}, u32[]{:S(2)}) copy-start(bf16[1,128,4096]{2,1,0:T(8,128)(2,1)} %param.10) | copy-start | bytes 3145732
  0.0 11.7 %collective-permute-start = (bf16[2,4096]{1,0:T(2,128)(2,1)}, bf16[2,4096]{1,0:T(2,128)(2,1)S(1)}, u32[]{:S(2)}, u32[]{:S(2)}) collective-permute-start(bf16[2,4096]{1,0:T(2,128)(2,1)} %bitcast.123), channel_id=1, source_target_pairs={{0,256},{256,0},{1,257},{257,1},{2,258},{258,2},{3,259},{259,3},{4... | collective-permute-start | bytes 49160 | tf_op jit(solution)/shard_map/ppermute | solution.py:18
  9.3 4.1 %copy-start.4 = (bf16[1,128,4096]{2,1,0:T(8,128)(2,1)S(1)}, bf16[1,128,4096]{2,1,0:T(8,128)(2,1)}, u32[]{:S(2)}) copy-start(bf16[1,128,4096]{2,1,0:T(8,128)(2,1)} %param.11) | copy-start | bytes 3145732
  13.4 1.2 copy-start.5
  17.9 13.3 %copy-start.7 = (bf16[1,256]{1,0:T(2,128)(2,1)S(1)}, bf16[1,256]{1,0:T(2,128)(2,1)}, u32[]{:S(2)}) copy-start(bf16[1,256]{1,0:T(2,128)(2,1)} %param.15) | copy-start | bytes 1540
  17.9 15.4 %copy-start.8 = (s32[2]{0:T(128)S(1)}, s32[2]{0:T(128)}, u32[]{:S(2)}) copy-start(s32[2]{0:T(128)} %param.17) | copy-start | bytes 28
  17.9 54.7 %all-to-all-start = ((bf16[1,3,128,16,256]{2,4,1,0,3:T(8,128)(2,1)}), bf16[1,3,128,16,256]{2,4,1,0,3:T(8,128)(2,1)S(1)}, u32[]{:S(2)}, u32[]{:S(2)}) async-start(bf16[1,3,128,16,256]{2,4,1,0,3:T(8,128)(2,1)} %pad_maximum_fusion), calls=%async_computation | async-start | bytes 6291456 | tf_op jit(solution)/shard_map/all_to_all | solution.py:50
  26.0 44.1 %collective-permute-start.2 = (bf16[2,2,128,256]{2,3,1,0:T(8,128)(2,1)S(1)}, bf16[2,2,128,256]{2,3,1,0:T(8,128)(2,1)}, u32[]{:S(2)}, u32[]{:S(2)}) collective-permute-start(bf16[2,2,128,256]{2,3,1,0:T(8,128)(2,1)S(1)} %bitcast.119), channel_id=1, source_target_pairs={{0,256},{256,0},{1,257},{257,1},{2,258},{258,2},{3,259},{259,3},{4... | collective-permute-start | bytes 786440 | tf_op jit(solution)/shard_map/ppermute | solution.py:18
  31.2 38.9 %collective-permute-start.1 = (bf16[256]{0:T(256)(128)(2,1)S(1)}, bf16[256]{0:T(256)(128)(2,1)S(1)}, u32[]{:S(2)}, u32[]{:S(2)}) collective-permute-start(bf16[256]{0:T(256)(128)(2,1)S(1)} %reduce.2), channel_id=1, source_target_pairs={{0,256},{256,0},{1,257},{257,1},{2,258},{258,2},{3,259},{259,3},{4... | collective-permute-start | bytes 1544 | tf_op jit(solution)/shard_map/ppermute | solution.py:18
  89.7 3.2 %copy-start = (f32[2,512,2048]{2,1,0:T(8,128)}, f32[2,512,2048]{2,1,0:T(8,128)S(1)}, u32[]{:S(2)}) copy-start(f32[2,512,2048]{2,1,0:T(8,128)S(1)} %fusion.93) | copy-start | bytes 25165828 | tf_op jit(solution)/shard_map/while
  108.8 0.8 copy-start.1
  111.1 0.8 copy-start.2
  123.1 3.2 %copy-start = (f32[2,512,2048]{2,1,0:T(8,128)}, f32[2,512,2048]{2,1,0:T(8,128)S(1)}, u32[]{:S(2)}) copy-start(f32[2,512,2048]{2,1,0:T(8,128)S(1)} %fusion.93) | copy-start | bytes 25165828 | tf_op jit(solution)/shard_map/while
  142.2 0.8 copy-start.1
  144.5 0.8 copy-start.2
  156.4 3.2 %copy-start = (f32[2,512,2048]{2,1,0:T(8,128)}, f32[2,512,2048]{2,1,0:T(8,128)S(1)}, u32[]{:S(2)}) copy-start(f32[2,512,2048]{2,1,0:T(8,128)S(1)} %fusion.93) | copy-start | bytes 25165828 | tf_op jit(solution)/shard_map/while
  175.6 0.8 copy-start.1
  177.9 0.8 copy-start.2
  189.8 3.2 %copy-start = (f32[2,512,2048]{2,1,0:T(8,128)}, f32[2,512,2048]{2,1,0:T(8,128)S(1)}, u32[]{:S(2)}) copy-start(f32[2,512,2048]{2,1,0:T(8,128)S(1)} %fusion.93) | copy-start | bytes 25165828 | tf_op jit(solution)/shard_map/while
  208.9 0.8 copy-start.1
  211.2 0.8 copy-start.2
where the time goes:
time: 244 us; the launch traced here: 243 us
  matrix products  73.3 us (30%)
  local copies, waits for them, and re-layouts  66.1 us (27%)
  waiting for transfers between devices  36.7 us (15%)
  blocking collectives  20.2 us (8%)
  starting transfers between devices  19.8 us (8%)
  other arithmetic  17.4 us (7%)
  loops' own time  8.63 us (4%)
    dot_general x12, matrix products, attend_block(): jnp.einsum('hrk,khd->rhd', probabilities, value_rows, preferred_element_t...  57.4 us
    ppermute x3, waiting for transfers between devices, swapped(): return lax.ppermute(value, axis, pairs)  36.7 us
    all_to_all x1, blocking collectives, teacher_slots(): lax.all_to_all(merged, 'seq', split_axis=1, concat_axis=3, tiled=True)  20.2 us
    while x24, local copies, waits for them, and re-layouts  19.2 us
    dot_general x12, matrix products, attend_block(): jnp.einsum('rhd,khd->hrk', query_rows, key_rows, preferred_element_type=j...  16 us
    ppermute x3, starting transfers between devices, swapped(): return lax.ppermute(value, axis, pairs)  12.8 us
    another operation x4, local copies, waits for them, and re-layouts  11.7 us
    sub x12, other arithmetic, attend_block(): weights = jnp.exp(scores - row_peak)  9.51 us
  transfers between devices with their start and end apart: 4, of which 1 were waited for; matrix products, arithmetic and copies ran while one was open for 4% of the time, Pallas kernels for 0%

commit v1 on v0

v1 whole, which is shorter than its diff:
```python
import functools
import math

import jax
import jax.numpy as jnp
from jax import lax
from jax.experimental import pallas as pl
from jax.experimental.pallas import tpu as pltpu
from jax.sharding import PartitionSpec as P

HEAD_DIM = 128
BOUNDARY = 875
GUIDANCE = 5.0
EPS = 1e-06
SCORE_SCALE = math.log2(math.e) / math.sqrt(HEAD_DIM)
MESH = pl.DeviceIdType.MESH
ROWS_OF_Y = 4
NT = (((1,), (1,)), ((), ()))


def place(me):
    return me // 4, (me // 2) % 2, me % 2


def source_of(me, i):
    y, x, core = place(me)
    chip = i // 2
    y, x, core = (y + chip // 2) % ROWS_OF_Y, (x + chip % 2) % 2, (core + i % 2) % 2
    return (y * 2 + x) * 2 + core


def target_of(me, i):
    y, x, core = place(me)
    chip = i // 2
    y, x, core = (y + ROWS_OF_Y - chip // 2) % ROWS_OF_Y, (x + chip % 2) % 2, (core + i % 2) % 2
    return (y * 2 + x) * 2 + core


def kernel(
    sizes,
    steps_ref, lengths_ref, q_ref, k_ref, v_ref, gain_ref, cross_gain_ref, prompt_ref,
    out_ref,
    q_rows, k_rows, gain_rows, cross_rows,
    q_got, k_got, v_got,
    k_normed, v_wide, out_blocks,
    scale_own, scale_got, k_scale, q_scale,
    gains, tables, cross_keys, cross_values,
    row_sems, q_sems, k_sems, v_sems, scale_sems, send_sems,
    out_sem, gain_sem, table_own_sem, piece_sem, table_sem,
):
    parts, groups, tok, cols = sizes
    expert = lax.axis_index("expert")
    dp = lax.axis_index("dp")
    me = lax.axis_index("seq")
    other = 1 - expert
    piece = tables.shape[1] // groups

    barrier = pltpu.get_barrier_semaphore()

    def greet_seq(i, carry):
        pl.semaphore_signal(barrier, 1, device_id={"seq": (me + i) % parts}, device_id_type=MESH)
        return carry

    def greet_dp(i, carry):
        pl.semaphore_signal(barrier, 1, device_id={"dp": (dp + i) % groups}, device_id_type=MESH)
        return carry

    lax.fori_loop(1, parts, greet_seq, 0)
    pl.semaphore_signal(barrier, 1, device_id={"expert": other}, device_id_type=MESH)
    lax.fori_loop(1, groups, greet_dp, 0)

    own_cols = pl.ds(pl.multiple_of(me * cols, cols), cols)
    local = [
        pltpu.make_async_copy(gain_ref, gain_rows, row_sems.at[0]),
        pltpu.make_async_copy(cross_gain_ref, cross_rows, row_sems.at[1]),
        pltpu.make_async_copy(k_ref, k_rows, row_sems.at[2]),
        pltpu.make_async_copy(q_ref, q_rows, row_sems.at[3]),
        pltpu.make_async_copy(prompt_ref, tables.at[0], table_own_sem),
        pltpu.make_async_copy(k_ref.at[:, own_cols], k_got.at[me], k_sems.at[me]),
        pltpu.make_async_copy(v_ref.at[:, own_cols], v_got.at[me], v_sems.at[me]),
        pltpu.make_async_copy(q_ref.at[:, own_cols], q_got.at[me], q_sems.at[me]),
    ]
    for copy in local:
        copy.start()
    v_wide[:, :, HEAD_DIM:] = jnp.ones((2, parts * tok, HEAD_DIM), jnp.bfloat16)

    pl.semaphore_wait(barrier, parts + groups - 1)

    def spread(src, got, sems, kind):
        def one(i, carry):
            d = target_of(me, i)
            theirs = pl.ds(pl.multiple_of(d * cols, cols), cols)
            pltpu.make_async_remote_copy(
                src_ref=src.at[:, theirs], dst_ref=got.at[me],
                send_sem=send_sems.at[kind], recv_sem=sems.at[me],
                device_id={"seq": d}, device_id_type=MESH,
            ).start()
            return carry

        lax.fori_loop(1, parts, one, 0)

    def await_bytes(ref, sem):
        pltpu.make_async_copy(ref, ref, sem).wait()

    spread(k_ref, k_got, k_sems, 0)

    mine = pl.ds(pl.multiple_of(dp * piece, piece), piece)
    fetch = pltpu.make_async_remote_copy(
        src_ref=prompt_ref.at[mine], dst_ref=tables.at[1, mine],
        send_sem=send_sems.at[5], recv_sem=piece_sem,
        device_id={"expert": other}, device_id_type=MESH,
    )
    fetch.start()

    local[0].wait()
    local[1].wait()
    gains[0, 0:2, :] = gain_rows[:, own_cols].astype(jnp.float32)
    gains[0, 2:3, :] = cross_rows[...].astype(jnp.float32)
    gains[0, 3:8, :] = jnp.zeros((5, cols), jnp.float32)
    swap = pltpu.make_async_remote_copy(
        src_ref=gains.at[0], dst_ref=gains.at[1],
        send_sem=send_sems.at[6], recv_sem=gain_sem,
        device_id={"expert": other}, device_id_type=MESH,
    )
    swap.start()

    def inverse_rms(rows):
        def add(c, total):
            part = rows[:, pl.ds(pl.multiple_of(c * 512, 512), 512)].astype(jnp.float32)
            part = part * part
            return total + (
                (part[:, :128] + part[:, 128:256]) + (part[:, 256:384] + part[:, 384:])
            )

        width = rows.shape[1]
        total = lax.fori_loop(0, width // 512, add, jnp.zeros((tok, 128), jnp.float32))
        mean = jnp.sum(jnp.transpose(total), axis=0, keepdims=True) / width
        return lax.rsqrt(mean + EPS)

    local[2].wait()
    scale_own[0:1, :] = inverse_rms(k_rows)
    local[3].wait()
    scale_own[1:2, :] = inverse_rms(q_rows)
    scale_own[2:8, :] = jnp.zeros((6, tok), jnp.float32)
    scale_got[me] = scale_own[...]

    def send_scale(i, carry):
        d = target_of(me, i)
        pltpu.make_async_remote_copy(
            src_ref=scale_own, dst_ref=scale_got.at[me],
            send_sem=send_sems.at[3], recv_sem=scale_sems.at[me],
            device_id={"seq": d}, device_id_type=MESH,
        ).start()
        return carry

    lax.fori_loop(1, parts, send_scale, 0)

    fetch.wait_recv()

    def pass_on(i, carry):
        pltpu.make_async_remote_copy(
            src_ref=tables.at[1, mine], dst_ref=tables.at[1, mine],
            send_sem=send_sems.at[7], recv_sem=table_sem,
            device_id={"dp": (dp + i) % groups}, device_id_type=MESH,
        ).start()
        return carry

    lax.fori_loop(1, groups, pass_on, 0)

    spread(v_ref, v_got, v_sems, 1)
    spread(q_ref, q_got, q_sems, 2)

    swap.wait_recv()

    def await_scale(i, carry):
        s = source_of(me, i)
        await_bytes(scale_got.at[s], scale_sems.at[s])
        return carry

    lax.fori_loop(1, parts, await_scale, 0)
    flipped = jnp.transpose(scale_got[...].reshape(parts * 8, tok))
    for s in range(parts):
        k_scale[s] = jnp.broadcast_to(flipped[:, 8 * s : 8 * s + 1], (tok, 128))
        q_scale[s] = jnp.broadcast_to(flipped[:, 8 * s + 1 : 8 * s + 2], (tok, 128))

    routed = jnp.where(steps_ref[0] >= BOUNDARY, 0, 1)
    choice = jnp.where(routed == expert, 0, 1)
    chosen = gains[choice]
    q_gain = chosen[0:1, :] * SCORE_SCALE
    k_gain = chosen[1:2, :]
    cross_gain = chosen[2:3, :] * SCORE_SCALE

    def take_keys(i, carry):
        s = source_of(me, i)
        await_bytes(k_got.at[s], k_sems.at[s])
        scale = k_scale[s]
        for h in range(2):
            lanes = slice(h * HEAD_DIM, (h + 1) * HEAD_DIM)
            normed = k_got[s, :, lanes].astype(jnp.float32) * scale * k_gain[:, lanes]
            k_normed[h, pl.ds(pl.multiple_of(s * tok, tok), tok), :] = normed.astype(jnp.bfloat16)
        return carry

    lax.fori_loop(0, parts, take_keys, 0)

    local[4].wait()
    fetch.wait_send()
    await_bytes(tables.at[1, pl.ds(0, piece * (groups - 1))], table_sem)
    for h in range(2):
        lanes = slice(h * HEAD_DIM, (h + 1) * HEAD_DIM)
        for b in range(2):
            rows = slice(b * 128, (b + 1) * 128)
            cross_keys[h, rows, :] = tables[choice, b * 256 : b * 256 + 128, lanes]
            cross_values[h, rows, :] = tables[choice, b * 256 + 128 : b * 256 + 256, lanes]

    def take_values(i, carry):
        s = source_of(me, i)
        await_bytes(v_got.at[s], v_sems.at[s])
        for h in range(2):
            lanes = slice(h * HEAD_DIM, (h + 1) * HEAD_DIM)
            v_wide[h, pl.ds(pl.multiple_of(s * tok, tok), tok), :HEAD_DIM] = v_got[s, :, lanes]
        return carry

    lax.fori_loop(0, parts, take_values, 0)

    position = lax.broadcasted_iota(jnp.int32, (2 * tok, 128), 1)
    visible = [position < lengths_ref[b] for b in range(2)]
    weight = (GUIDANCE, 1.0 - GUIDANCE)

    def attend(j, carry):
        s = (source_of(me, 2 * j) // 2) * 2
        for c in range(2):
            await_bytes(q_got.at[s + c], q_sems.at[s + c])
        pair = pl.ds(s, 2)
        scale = q_scale[pair].reshape(2 * tok, 128)
        for h in range(2):
            lanes = slice(h * HEAD_DIM, (h + 1) * HEAD_DIM)
            rows = q_got[pair, :, lanes].reshape(2 * tok, HEAD_DIM).astype(jnp.float32)
            query = (rows * scale * q_gain[:, lanes]).astype(jnp.bfloat16)
            scores = lax.dot_general(query, k_normed[h], NT, preferred_element_type=jnp.float32)
            peak = jnp.max(scores, axis=1, keepdims=True)
            weights = jnp.exp2(scores - peak).astype(jnp.bfloat16)
            sums = jnp.dot(weights, v_wide[h], preferred_element_type=jnp.float32)
            self_out = (sums[:, :HEAD_DIM] / sums[:, HEAD_DIM:]).astype(jnp.bfloat16)
            self_out = self_out.astype(jnp.float32)
            mean = jnp.mean(self_out * self_out, axis=1, keepdims=True)
            cross_query = self_out * lax.rsqrt(mean + EPS) * cross_gain[:, lanes]
            cross_scores = lax.dot_general(
                cross_query.astype(jnp.bfloat16), cross_keys[h], NT,
                preferred_element_type=jnp.float32,
            )
            shares = []
            for b in range(2):
                branch = jnp.where(
                    visible[b], cross_scores[:, b * 128 : (b + 1) * 128], -jnp.inf
                )
                branch = jnp.exp2(branch - jnp.max(branch, axis=1, keepdims=True))
                factor = weight[b] / jnp.sum(branch, axis=1, keepdims=True)
                shares.append((branch * factor).astype(jnp.bfloat16))
            guided = self_out + jnp.dot(
                jnp.concatenate(shares, axis=1), cross_values[h],
                preferred_element_type=jnp.float32,
            )
            out_blocks[pair, :, lanes] = guided.astype(jnp.bfloat16).reshape(2, tok, HEAD_DIM)
        for c in range(2):
            d = s + c

            @pl.when(d != me)
            def _():
                pltpu.make_async_remote_copy(
                    src_ref=out_blocks.at[d], dst_ref=out_ref.at[:, own_cols],
                    send_sem=send_sems.at[4], recv_sem=out_sem,
                    device_id={"seq": d}, device_id_type=MESH,
                ).start()

            @pl.when(d == me)
            def _():
                pltpu.make_async_copy(out_blocks.at[d], out_ref.at[:, own_cols], out_sem).start()

        return carry

    lax.fori_loop(0, parts // 2, attend, 0)

    swap.wait_send()
    some = pl.ds(0, parts - 1)
    await_bytes(k_got.at[some], send_sems.at[0])
    await_bytes(v_got.at[some], send_sems.at[1])
    await_bytes(q_got.at[some], send_sems.at[2])
    await_bytes(scale_got.at[some], send_sems.at[3])
    await_bytes(tables.at[1, pl.ds(0, piece * (groups - 1))], send_sems.at[7])
    await_bytes(out_blocks.at[some], send_sems.at[4])
    await_bytes(out_ref, out_sem)


def body(q, k, v, timesteps, norm_gain, cross_gain, prompts, lengths):
    parts, groups = lax.axis_size("seq"), lax.axis_size("dp")
    _, tok, width = q.shape
    cols = width // parts
    text = prompts.shape[3]
    bf16, f32 = jnp.bfloat16, jnp.float32
    hbm = pl.BlockSpec(memory_space=pltpu.HBM)
    smem = pl.BlockSpec(memory_space=pltpu.SMEM)
    dma = pltpu.SemaphoreType.DMA
    out = pl.pallas_call(
        functools.partial(kernel, (parts, groups, tok, cols)),
        out_shape=jax.ShapeDtypeStruct((tok, width), bf16),
        in_specs=[smem, smem] + [hbm] * 6,
        out_specs=hbm,
        scratch_shapes=[
            pltpu.VMEM((tok, width), bf16),
            pltpu.VMEM((tok, width), bf16),
            pltpu.VMEM((2, width), bf16),
            pltpu.VMEM((1, cols), bf16),
            pltpu.VMEM((parts, tok, cols), bf16),
            pltpu.VMEM((parts, tok, cols), bf16),
            pltpu.VMEM((parts, tok, cols), bf16),
            pltpu.VMEM((2, parts * tok, HEAD_DIM), bf16),
            pltpu.VMEM((2, parts * tok, 2 * HEAD_DIM), bf16),
            pltpu.VMEM((parts, tok, cols), bf16),
            pltpu.VMEM((8, tok), f32),
            pltpu.VMEM((parts, 8, tok), f32),
            pltpu.VMEM((parts, tok, 128), f32),
            pltpu.VMEM((parts, tok, 128), f32),
            pltpu.VMEM((2, 8, cols), f32),
            pltpu.VMEM((2, 4 * text, cols), bf16),
            pltpu.VMEM((2, 2 * text, HEAD_DIM), bf16),
            pltpu.VMEM((2, 2 * text, HEAD_DIM), bf16),
            dma((4,)),
            dma((parts,)),
            dma((parts,)),
            dma((parts,)),
            dma((parts,)),
            dma((8,)),
            dma,
            dma,
            dma,
            dma,
            dma,
        ],
        compiler_params=pltpu.CompilerParams(
            collective_id=0, has_side_effects=True, vmem_limit_bytes=63 * 2**20
        ),
        name="guided_attention",
    )(
        timesteps, lengths,
        q.reshape(tok, width), k.reshape(tok, width), v.reshape(tok, width),
        norm_gain.reshape(2, width), cross_gain, prompts.reshape(4 * text, cols),
    )
    return out[None]


def solution(mesh):
    placed = (
        P(("expert", "dp"), "seq", None),
        P(("expert", "dp"), "seq", None),
        P(("expert", "dp"), "seq", None),
        P(("expert", "dp")),
        P("expert", None, None),
        P("expert", "seq"),
        P("expert", None, None, None, "seq"),
        P(),
    )
    return jax.shard_map(
        body,
        mesh=mesh,
        in_specs=placed,
        out_specs=P(("expert", "dp"), "seq", None),
        check_vma=False,
    )
```

time: 244 us -> 85.2 us (0.35)
  Pallas kernels: 0 us -> 82.1 us
  matrix products: 73.3 us -> 0 us
  local copies, waits for them, and re-layouts: 66.1 us -> 2.29 us
  waiting for transfers between devices: 36.7 us -> 0 us
  blocking collectives: 20.2 us -> 0 us
  starting transfers between devices: 19.8 us -> 0 us
  other arithmetic: 17.4 us -> 0 us
  loops' own time: 8.63 us -> 0 us
    pallas_call x0 -> x1, Pallas kernels: none -> 82.1 us  [body(): pl.pallas_call(functools.partial(kernel, (parts, groups, tok, cols)), out...]
    dot_general x24 -> x0, matrix products: 73.3 us -> none  [the longest x12 57.4 us: attend_block(): jnp.einsum('hrk,khd->rhd', probabilities, value_rows, preferred_element_t...]
    ppermute x3 -> x0, waiting for transfers between devices: 36.7 us -> none  [swapped(): return lax.ppermute(value, axis, pairs)]
    while x26 -> x0, local copies, waits for them, and re-layouts: 24.5 us -> none
    all_to_all x1 -> x0, blocking collectives: 20.2 us -> none  [teacher_slots(): lax.all_to_all(merged, 'seq', split_axis=1, concat_axis=3, tiled=True)]
    another operation x6 -> x0, local copies, waits for them, and re-layouts: 14.8 us -> none
    ppermute x3 -> x0, starting transfers between devices: 12.8 us -> none  [swapped(): return lax.ppermute(value, axis, pairs)]
    sub x12 -> x0, other arithmetic: 9.51 us -> none  [attend_block(): weights = jnp.exp(scores - row_peak)]
  transfers between devices with their start and end apart: 4 -> 0, of which waited for: 1 -> 0; matrix products, arithmetic and copies ran while one was open for 4% -> 0% of each run, Pallas kernels for 0% -> 0%
where the time goes in v1:
time: 85.2 us; the launch traced here: 85 us
  Pallas kernels  82.1 us (96%)
  local copies, waits for them, and re-layouts  2.29 us (3%)
    pallas_call x1, Pallas kernels, body(): pl.pallas_call(functools.partial(kernel, (parts, groups, tok, cols)), out...  82.1 us
    unnamed x1, local copies, waits for them, and re-layouts  2.29 us

profile of v1, /device:TPU:1, one launch (start us, length us, event | category | flops | bytes accessed | tf_op | source)
XLA Modules:
  0.0 85.0 jit_solution(13909972479724376216)
XLA Ops:
  0.7 82.1 %guided_attention.1 = bf16[128,4096]{1,0:T(8,128)(2,1)} custom-call(s32[1]{0:T(128)S(6)} %copy.10.steps_ref, s32[2]{0:T(128)} %lengths_ref.1, bf16[128,4096]{1,0:T(8,128)(2,1)} %bitcast.7, bf16[128,4096]{1,0:T(8,128)(2,1)} %bitcast.8, bf16[128,4096]{1,0:T(8,128)(2,1)} %bitcast.9, bf16[2,4096]{1,0:T(2,128)(2,1)} %bitcast.11, bf16[1,256]{1,0:T(2,128)(2,1)} %cross_gain_ref.1, ...), custom_call_target="tpu_custom_call" | custom-call | tf_op jit(solution)/shard_map/guided_attention/pallas_call | solution.py:303
  82.8 2.3 %copy.11 = bf16[1,128,4096]{2,1,0:T(8,128)(2,1)} copy(bf16[1,128,4096]{2,1,0:T(8,128)(2,1)} %bitcast.6) | data formatting | bytes 2097152

commit v2 on v1

v2 whole, which is shorter than its diff:
```python
import functools
import math

import jax
import jax.numpy as jnp
from jax import lax
from jax.experimental import pallas as pl
from jax.experimental.pallas import tpu as pltpu
from jax.sharding import PartitionSpec as P

HEAD_DIM = 128
BOUNDARY = 875
GUIDANCE = 5.0
EPS = 1e-06
SCORE_SCALE = math.log2(math.e) / math.sqrt(HEAD_DIM)
MESH = pl.DeviceIdType.MESH
ROWS_OF_Y = 4
NT = (((1,), (1,)), ((), ()))


def place(me):
    return me // 4, (me // 2) % 2, me % 2


def source_of(me, i):
    y, x, core = place(me)
    chip = i // 2
    y, x, core = (y + chip // 2) % ROWS_OF_Y, (x + chip % 2) % 2, (core + i % 2) % 2
    return (y * 2 + x) * 2 + core


def target_of(me, i):
    y, x, core = place(me)
    chip = i // 2
    y, x, core = (y + ROWS_OF_Y - chip // 2) % ROWS_OF_Y, (x + chip % 2) % 2, (core + i % 2) % 2
    return (y * 2 + x) * 2 + core


def kernel(
    sizes,
    steps_ref, lengths_ref, q_ref, k_ref, v_ref, gain_ref, cross_gain_ref, prompt_ref,
    out_ref,
    q_rows, k_rows, v_rows, gain_rows, cross_rows,
    q_sent, k_sent, v_sent,
    q_got, k_got, v_got,
    k_normed, v_wide, out_blocks, out_got,
    scale_own, scale_got, k_scale, q_scale,
    gains, tables, cross_keys, cross_values,
    row_sems, q_sems, k_sems, v_sems, scale_sems, send_sems,
    out_sem, gain_sem, table_own_sem, table_sem,
):
    parts, tok, cols = sizes
    expert = lax.axis_index("expert")
    me = lax.axis_index("seq")

    def across(d):
        return d + 2 - 4 * ((d // 2) % 2)

    routed = jnp.where(steps_ref[0] >= BOUNDARY, 0, 1)
    choice = jnp.where(routed == expert, 0, 1)

    def pick(here, there):
        return lax.select_n(choice == 1, here, there)

    partner = {"expert": 1 - expert, "seq": across(me)}

    barrier = pltpu.get_barrier_semaphore()

    def greet(i, carry):
        pl.semaphore_signal(barrier, 1, device_id={"seq": (me + i) % parts}, device_id_type=MESH)
        return carry

    lax.fori_loop(1, parts, greet, 0)
    pl.semaphore_signal(barrier, 1, device_id=partner, device_id_type=MESH)

    own_cols = pl.ds(pl.multiple_of(me * cols, cols), cols)
    local = [
        pltpu.make_async_copy(k_ref, k_rows, row_sems.at[0]),
        pltpu.make_async_copy(gain_ref, gain_rows, row_sems.at[1]),
        pltpu.make_async_copy(cross_gain_ref, cross_rows, row_sems.at[2]),
        pltpu.make_async_copy(q_ref, q_rows, row_sems.at[3]),
        pltpu.make_async_copy(v_ref, v_rows, row_sems.at[4]),
        pltpu.make_async_copy(prompt_ref, tables.at[0], table_own_sem),
    ]
    for copy in local:
        copy.start()

    def stage(rows, sent):
        def one(d, carry):
            here = pl.ds(pl.multiple_of(d * cols, cols), cols)
            there = pl.ds(pl.multiple_of(across(d) * cols, cols), cols)
            sent[d] = pick(rows[:, here], rows[:, there])
            return carry

        lax.fori_loop(0, parts, one, 0)

    def spread(sent, got, sems, kind):
        def one(i, carry):
            d = target_of(me, i)
            pltpu.make_async_remote_copy(
                src_ref=sent.at[d], dst_ref=got.at[me],
                send_sem=send_sems.at[kind], recv_sem=sems.at[me],
                device_id={"seq": d}, device_id_type=MESH,
            ).start()
            return carry

        lax.fori_loop(1, parts, one, 0)

    def await_bytes(ref, sem):
        pltpu.make_async_copy(ref, ref, sem).wait()

    local[0].wait()
    stage(k_rows, k_sent)
    pl.semaphore_wait(barrier, parts)
    spread(k_sent, k_got, k_sems, 0)

    local[1].wait()
    local[2].wait()
    gains[0, 0:2, :] = gain_rows[:, own_cols].astype(jnp.float32)
    gains[0, 2:3, :] = cross_rows[...].astype(jnp.float32)
    gains[0, 3:8, :] = jnp.zeros((5, cols), jnp.float32)
    swap = pltpu.make_async_remote_copy(
        src_ref=gains.at[0], dst_ref=gains.at[1],
        send_sem=send_sems.at[6], recv_sem=gain_sem,
        device_id=partner, device_id_type=MESH,
    )
    swap.start()
    fetch = pltpu.make_async_remote_copy(
        src_ref=prompt_ref, dst_ref=tables.at[1],
        send_sem=send_sems.at[5], recv_sem=table_sem,
        device_id=partner, device_id_type=MESH,
    )
    fetch.start()

    def inverse_rms(rows):
        def add(c, total):
            part = rows[:, pl.ds(pl.multiple_of(c * 512, 512), 512)].astype(jnp.float32)
            part = part * part
            return total + (
                (part[:, :128] + part[:, 128:256]) + (part[:, 256:384] + part[:, 384:])
            )

        width = rows.shape[1]
        total = lax.fori_loop(0, width // 512, add, jnp.zeros((tok, 128), jnp.float32))
        mean = jnp.sum(jnp.transpose(total), axis=0, keepdims=True) / width
        return lax.rsqrt(mean + EPS)

    scale_own[0:1, :] = inverse_rms(k_rows)
    local[3].wait()
    scale_own[1:2, :] = inverse_rms(q_rows)
    scale_own[2:8, :] = jnp.zeros((6, tok), jnp.float32)
    scale_got[me] = scale_own[...]

    def send_scale(i, carry):
        d = target_of(me, i)
        pltpu.make_async_remote_copy(
            src_ref=scale_own, dst_ref=scale_got.at[me],
            send_sem=send_sems.at[3], recv_sem=scale_sems.at[me],
            device_id={"seq": d}, device_id_type=MESH,
        ).start()
        return carry

    lax.fori_loop(1, parts, send_scale, 0)

    local[4].wait()
    stage(v_rows, v_sent)
    spread(v_sent, v_got, v_sems, 1)
    stage(q_rows, q_sent)
    spread(q_sent, q_got, q_sems, 2)
    k_got[me] = k_sent[me]
    v_got[me] = v_sent[me]
    q_got[me] = q_sent[me]
    v_wide[:, :, HEAD_DIM:] = jnp.ones((2, parts * tok, HEAD_DIM), jnp.bfloat16)

    swap.wait_recv()

    def await_scale(i, carry):
        s = source_of(me, i)
        await_bytes(scale_got.at[s], scale_sems.at[s])
        return carry

    lax.fori_loop(1, parts, await_scale, 0)
    flipped = jnp.transpose(scale_got[...].reshape(parts * 8, tok))
    for s in range(parts):
        k_scale[s] = jnp.broadcast_to(flipped[:, 8 * s : 8 * s + 1], (tok, 128))
        q_scale[s] = jnp.broadcast_to(flipped[:, 8 * s + 1 : 8 * s + 2], (tok, 128))

    chosen = gains[choice]
    q_gain = chosen[0:1, :] * SCORE_SCALE
    k_gain = chosen[1:2, :]
    cross_gain = chosen[2:3, :] * SCORE_SCALE

    def take_keys(i, carry):
        s = source_of(me, i)

        @pl.when(i > 0)
        def _():
            await_bytes(k_got.at[s], k_sems.at[s])

        scale = k_scale[s]
        for h in range(2):
            lanes = slice(h * HEAD_DIM, (h + 1) * HEAD_DIM)
            normed = k_got[s, :, lanes].astype(jnp.float32) * scale * k_gain[:, lanes]
            k_normed[h, pl.ds(pl.multiple_of(s * tok, tok), tok), :] = normed.astype(jnp.bfloat16)
        return carry

    lax.fori_loop(0, parts, take_keys, 0)

    local[5].wait()
    fetch.wait_recv()
    for h in range(2):
        lanes = slice(h * HEAD_DIM, (h + 1) * HEAD_DIM)
        for b in range(2):
            rows = slice(b * 128, (b + 1) * 128)
            cross_keys[h, rows, :] = tables[choice, b * 256 : b * 256 + 128, lanes]
            cross_values[h, rows, :] = tables[choice, b * 256 + 128 : b * 256 + 256, lanes]

    def take_values(i, carry):
        s = source_of(me, i)

        @pl.when(i > 0)
        def _():
            await_bytes(v_got.at[s], v_sems.at[s])

        for h in range(2):
            lanes = slice(h * HEAD_DIM, (h + 1) * HEAD_DIM)
            v_wide[h, pl.ds(pl.multiple_of(s * tok, tok), tok), :HEAD_DIM] = v_got[s, :, lanes]
        return carry

    lax.fori_loop(0, parts, take_values, 0)

    position = lax.broadcasted_iota(jnp.int32, (2 * tok, 128), 1)
    visible = [position < lengths_ref[b] for b in range(2)]
    weight = (GUIDANCE, 1.0 - GUIDANCE)

    def self_scores(pair, h):
        lanes = slice(h * HEAD_DIM, (h + 1) * HEAD_DIM)
        rows = q_got[pair, :, lanes].reshape(2 * tok, HEAD_DIM).astype(jnp.float32)
        scale = q_scale[pair].reshape(2 * tok, 128)
        query = (rows * scale * q_gain[:, lanes]).astype(jnp.bfloat16)
        return lax.dot_general(query, k_normed[h], NT, preferred_element_type=jnp.float32)

    def softmax_weights(scores):
        peak = jnp.max(scores, axis=1, keepdims=True)
        return jnp.exp2(scores - peak).astype(jnp.bfloat16)

    def self_values(weights, h):
        sums = jnp.dot(weights, v_wide[h], preferred_element_type=jnp.float32)
        self_out = (sums[:, :HEAD_DIM] / sums[:, HEAD_DIM:]).astype(jnp.bfloat16)
        return self_out.astype(jnp.float32)

    def cross_scores(self_out, h):
        lanes = slice(h * HEAD_DIM, (h + 1) * HEAD_DIM)
        mean = jnp.mean(self_out * self_out, axis=1, keepdims=True)
        query = self_out * lax.rsqrt(mean + EPS) * cross_gain[:, lanes]
        return lax.dot_general(
            query.astype(jnp.bfloat16), cross_keys[h], NT, preferred_element_type=jnp.float32
        )

    def cross_weights(scores):
        shares = []
        for b in range(2):
            branch = jnp.where(visible[b], scores[:, b * 128 : (b + 1) * 128], -jnp.inf)
            branch = jnp.exp2(branch - jnp.max(branch, axis=1, keepdims=True))
            factor = weight[b] / jnp.sum(branch, axis=1, keepdims=True)
            shares.append((branch * factor).astype(jnp.bfloat16))
        return jnp.concatenate(shares, axis=1)

    def attend(j, carry):
        s = (source_of(me, 2 * j) // 2) * 2
        for c in range(2):

            @pl.when(s + c != me)
            def _():
                await_bytes(q_got.at[s + c], q_sems.at[s + c])

        pair = pl.ds(s, 2)
        heads = range(2)
        scores = [self_scores(pair, h) for h in heads]
        weights = [softmax_weights(scores[h]) for h in heads]
        self_out = [self_values(weights[h], h) for h in heads]
        scores = [cross_scores(self_out[h], h) for h in heads]
        shares = [cross_weights(scores[h]) for h in heads]
        for h in heads:
            lanes = slice(h * HEAD_DIM, (h + 1) * HEAD_DIM)
            guided = self_out[h] + jnp.dot(
                shares[h], cross_values[h], preferred_element_type=jnp.float32
            )
            out_blocks[pair, :, lanes] = guided.astype(jnp.bfloat16).reshape(2, tok, HEAD_DIM)
        for c in range(2):
            d = s + c

            @pl.when(d != me)
            def _():
                pltpu.make_async_remote_copy(
                    src_ref=out_blocks.at[d], dst_ref=out_got.at[me],
                    send_sem=send_sems.at[4], recv_sem=out_sem,
                    device_id={"seq": d}, device_id_type=MESH,
                ).start()

            @pl.when(d == me)
            def _():
                out_got[me] = out_blocks[me]

        return carry

    lax.fori_loop(0, parts // 2, attend, 0)

    swap.wait_send()
    fetch.wait_send()
    some = pl.ds(0, parts - 1)
    await_bytes(k_got.at[some], send_sems.at[0])
    await_bytes(v_got.at[some], send_sems.at[1])
    await_bytes(q_got.at[some], send_sems.at[2])
    await_bytes(scale_got.at[some], send_sems.at[3])
    await_bytes(out_blocks.at[some], send_sems.at[4])
    await_bytes(out_got.at[some], out_sem)

    for d in range(parts):
        out_ref[:, d * cols : (d + 1) * cols] = pick(out_got[d], out_got[across(d)])


def body(q, k, v, timesteps, norm_gain, cross_gain, prompts, lengths):
    parts = lax.axis_size("seq")
    _, tok, width = q.shape
    cols = width // parts
    text = prompts.shape[3]
    bf16, f32 = jnp.bfloat16, jnp.float32
    hbm = pl.BlockSpec(memory_space=pltpu.HBM)
    smem = pl.BlockSpec(memory_space=pltpu.SMEM)
    dma = pltpu.SemaphoreType.DMA
    blocks = pltpu.VMEM((parts, tok, cols), bf16)
    out = pl.pallas_call(
        functools.partial(kernel, (parts, tok, cols)),
        out_shape=jax.ShapeDtypeStruct((tok, width), bf16),
        in_specs=[smem, smem] + [hbm] * 6,
        out_specs=pl.BlockSpec(memory_space=pltpu.VMEM),
        scratch_shapes=[
            pltpu.VMEM((tok, width), bf16),
            pltpu.VMEM((tok, width), bf16),
            pltpu.VMEM((tok, width), bf16),
            pltpu.VMEM((2, width), bf16),
            pltpu.VMEM((1, cols), bf16),
            blocks, blocks, blocks,
            blocks, blocks, blocks,
            pltpu.VMEM((2, parts * tok, HEAD_DIM), bf16),
            pltpu.VMEM((2, parts * tok, 2 * HEAD_DIM), bf16),
            blocks, blocks,
            pltpu.VMEM((8, tok), f32),
            pltpu.VMEM((parts, 8, tok), f32),
            pltpu.VMEM((parts, tok, 128), f32),
            pltpu.VMEM((parts, tok, 128), f32),
            pltpu.VMEM((2, 8, cols), f32),
            pltpu.VMEM((2, 4 * text, cols), bf16),
            pltpu.VMEM((2, 2 * text, HEAD_DIM), bf16),
            pltpu.VMEM((2, 2 * text, HEAD_DIM), bf16),
            dma((5,)),
            dma((parts,)),
            dma((parts,)),
            dma((parts,)),
            dma((parts,)),
            dma((7,)),
            dma,
            dma,
            dma,
            dma,
        ],
        compiler_params=pltpu.CompilerParams(
            collective_id=0, has_side_effects=True, vmem_limit_bytes=63 * 2**20
        ),
        name="guided_attention",
    )(
        timesteps, lengths,
        q.reshape(tok, width), k.reshape(tok, width), v.reshape(tok, width),
        norm_gain.reshape(2, width), cross_gain, prompts.reshape(4 * text, cols),
    )
    return out[None]


def solution(mesh):
    placed = (
        P(("expert", "dp"), "seq", None),
        P(("expert", "dp"), "seq", None),
        P(("expert", "dp"), "seq", None),
        P(("expert", "dp")),
        P("expert", None, None),
        P("expert", "seq"),
        P("expert", None, None, None, "seq"),
        P(),
    )
    return jax.shard_map(
        body,
        mesh=mesh,
        in_specs=placed,
        out_specs=P(("expert", "dp"), "seq", None),
        check_vma=False,
    )
```

time: 85.2 us -> 67.1 us (0.79)
  Pallas kernels: 82.1 us -> 64 us
    pallas_call x1, Pallas kernels: 82.1 us -> 64 us  [body(): pl.pallas_call(functools.partial(kernel, (parts, tok, cols)), out_shape=j...]
where the time goes in v2:
time: 67.1 us; the launch traced here: 67 us
  Pallas kernels  64 us (95%)
  local copies, waits for them, and re-layouts  2.29 us (3%)
    pallas_call x1, Pallas kernels, body(): pl.pallas_call(functools.partial(kernel, (parts, tok, cols)), out_shape=j...  64 us
    unnamed x1, local copies, waits for them, and re-layouts  2.29 us

profile of v2, /device:TPU:1, one launch (start us, length us, event | category | flops | bytes accessed | tf_op | source)
XLA Modules:
  0.0 67.0 jit_solution(7784837774577273519)
XLA Ops:
  0.7 64.0 %guided_attention.1 = bf16[128,4096]{1,0:T(8,128)(2,1)} custom-call(s32[1]{0:T(128)S(6)} %copy.10.steps_ref, s32[2]{0:T(128)} %lengths_ref.1, bf16[128,4096]{1,0:T(8,128)(2,1)} %bitcast.7, bf16[128,4096]{1,0:T(8,128)(2,1)} %bitcast.8, bf16[128,4096]{1,0:T(8,128)(2,1)} %bitcast.9, bf16[2,4096]{1,0:T(2,128)(2,1)} %bitcast.11, bf16[1,256]{1,0:T(2,128)(2,1)} %cross_gain_ref.1, ...), custom_call_target="tpu_custom_call" | custom-call | tf_op jit(solution)/shard_map/guided_attention/pallas_call | solution.py:333
  64.7 2.3 %copy.11 = bf16[1,128,4096]{2,1,0:T(8,128)(2,1)} copy(bf16[1,128,4096]{2,1,0:T(8,128)(2,1)} %bitcast.6) | data formatting | bytes 2097152

commit v3 on v2

--- a/solution.py
+++ b/solution.py
@@ -18,22 +18,39 @@
 NT = (((1,), (1,)), ((), ()))
 
 
-def place(me):
-    return me // 4, (me // 2) % 2, me % 2
-
-
-def source_of(me, i):
-    y, x, core = place(me)
-    chip = i // 2
-    y, x, core = (y + chip // 2) % ROWS_OF_Y, (x + chip % 2) % 2, (core + i % 2) % 2
+CHIPS = (5, 3, 7, 4, 1, 2, 6, 0)
+CHIP_CODE = sum(chip * 8**i for i, chip in enumerate(CHIPS))
+
+
+def over_chips(count, visit):
+    def step(_, code):
+        visit(code % 8)
+        return code // 8
+
+    lax.fori_loop(0, count, step, jnp.int32(CHIP_CODE))
+
+
+def shifted(me, y_steps, x_steps, core_steps):
+    y, x, core = me // 4, (me // 2) % 2, me % 2
+    y, x, core = (y + y_steps) % ROWS_OF_Y, (x + x_steps) % 2, (core + core_steps) % 2
     return (y * 2 + x) * 2 + core
 
 
-def target_of(me, i):
-    y, x, core = place(me)
-    chip = i // 2
-    y, x, core = (y + ROWS_OF_Y - chip // 2) % ROWS_OF_Y, (x + chip % 2) % 2, (core + i % 2) % 2
-    return (y * 2 + x) * 2 + core
+def source_of(me, chip, core_steps):
+    return shifted(me, chip // 2, chip % 2, core_steps)
+
+
+def target_of(me, chip, core_steps):
+    return shifted(me, ROWS_OF_Y - chip // 2, chip % 2, core_steps)
+
+
+def across(d):
+    return d + 2 - 4 * ((d // 2) % 2)
+
+
+def choice_of(steps_ref):
+    routed = jnp.where(steps_ref[0] >= BOUNDARY, 0, 1)
+    return jnp.where(routed == lax.axis_index("expert"), 0, 1)
 
 
 def kernel(
@@ -43,21 +60,17 @@
     q_rows, k_rows, v_rows, gain_rows, cross_rows,
     q_sent, k_sent, v_sent,
     q_got, k_got, v_got,
-    k_normed, v_wide, out_blocks, out_got,
+    k_normed, v_wide, out_blocks,
     scale_own, scale_got, k_scale, q_scale,
     gains, tables, cross_keys, cross_values,
     row_sems, q_sems, k_sems, v_sems, scale_sems, send_sems,
-    out_sem, gain_sem, table_own_sem, table_sem,
+    out_sem, gain_sem, table_own_sem, table_sem, late_sem, late_partner_sem,
 ):
     parts, tok, cols = sizes
     expert = lax.axis_index("expert")
     me = lax.axis_index("seq")
 
-    def across(d):
-        return d + 2 - 4 * ((d // 2) % 2)
-
-    routed = jnp.where(steps_ref[0] >= BOUNDARY, 0, 1)
-    choice = jnp.where(routed == expert, 0, 1)
+    choice = choice_of(steps_ref)
 
     def pick(here, there):
         return lax.select_n(choice == 1, here, there)
@@ -66,12 +79,19 @@
 
     barrier = pltpu.get_barrier_semaphore()
 
-    def greet(i, carry):
-        pl.semaphore_signal(barrier, 1, device_id={"seq": (me + i) % parts}, device_id_type=MESH)
-        return carry
-
-    lax.fori_loop(1, parts, greet, 0)
-    pl.semaphore_signal(barrier, 1, device_id=partner, device_id_type=MESH)
+    def signal_group(sem):
+        def one(i, carry):
+            pl.semaphore_signal(sem, 1, device_id={"seq": (me + i) % parts}, device_id_type=MESH)
+            return carry
+
+        lax.fori_loop(1, parts, one, 0)
+
+    scale_got[...] = jnp.zeros_like(scale_got)
+
+    @pl.when(me != 0)
+    def _():
+        signal_group(barrier)
+        pl.semaphore_signal(barrier, 1, device_id=partner, device_id_type=MESH)
 
     own_cols = pl.ds(pl.multiple_of(me * cols, cols), cols)
     local = [
@@ -94,25 +114,82 @@
 
         lax.fori_loop(0, parts, one, 0)
 
-    def spread(sent, got, sems, kind):
-        def one(i, carry):
-            d = target_of(me, i)
+    def to_group(send):
+        def chip(c):
+            for core in range(2):
+                send(target_of(me, c, core))
+
+        over_chips(parts // 2 - 1, chip)
+        send(shifted(me, 0, 0, 1))
+
+    def sender(sent, got, sems, kind):
+        def send(d):
             pltpu.make_async_remote_copy(
                 src_ref=sent.at[d], dst_ref=got.at[me],
                 send_sem=send_sems.at[kind], recv_sem=sems.at[me],
                 device_id={"seq": d}, device_id_type=MESH,
             ).start()
-            return carry
-
-        lax.fori_loop(1, parts, one, 0)
+
+        return send
+
+    def send_scale(d):
+        pltpu.make_async_remote_copy(
+            src_ref=scale_own.at[0:2], dst_ref=scale_got.at[me, 0:2],
+            send_sem=send_sems.at[3], recv_sem=scale_sems.at[me],
+            device_id={"seq": d}, device_id_type=MESH,
+        ).start()
+
+    def but_first(send):
+        def guarded(d):
+            @pl.when(d != 0)
+            def _():
+                send(d)
+
+        return guarded
 
     def await_bytes(ref, sem):
         pltpu.make_async_copy(ref, ref, sem).wait()
 
     local[0].wait()
     stage(k_rows, k_sent)
-    pl.semaphore_wait(barrier, parts)
-    spread(k_sent, k_got, k_sems, 0)
+
+    @pl.when(me == 0)
+    def _():
+        pl.semaphore_wait(barrier, parts)
+        signal_group(late_sem)
+        pl.semaphore_signal(late_partner_sem, 1, device_id=partner, device_id_type=MESH)
+
+    @pl.when(me == 2)
+    def _():
+        pl.semaphore_wait(barrier, parts - 2)
+
+    @pl.when((me != 0) & (me != 2))
+    def _():
+        pl.semaphore_wait(barrier, parts - 1)
+
+    send_keys = sender(k_sent, k_got, k_sems, 0)
+    to_group(but_first(send_keys))
+
+    def inverse_rms(rows):
+        def add(c, total):
+            part = rows[:, pl.ds(pl.multiple_of(c * 512, 512), 512)].astype(jnp.float32)
+            part = part * part
+            return total + (
+                (part[:, :128] + part[:, 128:256]) + (part[:, 256:384] + part[:, 384:])
+            )
+
+        width = rows.shape[1]
+        total = lax.fori_loop(0, width // 512, add, jnp.zeros((tok, 128), jnp.float32))
+        mean = jnp.sum(jnp.transpose(total), axis=0, keepdims=True) / width
+        return lax.rsqrt(mean + EPS)
+
+    scale_own[0:1, :] = inverse_rms(k_rows)
+    local[3].wait()
+    scale_own[1:2, :] = inverse_rms(q_rows)
+    scale_own[2:8, :] = jnp.zeros((6, tok), jnp.float32)
+    scale_got[me] = scale_own[...]
+
+    to_group(but_first(send_scale))
 
     local[1].wait()
     local[2].wait()
@@ -124,49 +201,29 @@
         send_sem=send_sems.at[6], recv_sem=gain_sem,
         device_id=partner, device_id_type=MESH,
     )
-    swap.start()
     fetch = pltpu.make_async_remote_copy(
         src_ref=prompt_ref, dst_ref=tables.at[1],
         send_sem=send_sems.at[5], recv_sem=table_sem,
         device_id=partner, device_id_type=MESH,
     )
-    fetch.start()
-
-    def inverse_rms(rows):
-        def add(c, total):
-            part = rows[:, pl.ds(pl.multiple_of(c * 512, 512), 512)].astype(jnp.float32)
-            part = part * part
-            return total + (
-                (part[:, :128] + part[:, 128:256]) + (part[:, 256:384] + part[:, 384:])
-            )
-
-        width = rows.shape[1]
-        total = lax.fori_loop(0, width // 512, add, jnp.zeros((tok, 128), jnp.float32))
-        mean = jnp.sum(jnp.transpose(total), axis=0, keepdims=True) / width
-        return lax.rsqrt(mean + EPS)
-
-    scale_own[0:1, :] = inverse_rms(k_rows)
-    local[3].wait()
-    scale_own[1:2, :] = inverse_rms(q_rows)
-    scale_own[2:8, :] = jnp.zeros((6, tok), jnp.float32)
-    scale_got[me] = scale_own[...]
-
-    def send_scale(i, carry):
-        d = target_of(me, i)
-        pltpu.make_async_remote_copy(
-            src_ref=scale_own, dst_ref=scale_got.at[me],
-            send_sem=send_sems.at[3], recv_sem=scale_sems.at[me],
-            device_id={"seq": d}, device_id_type=MESH,
-        ).start()
-        return carry
-
-    lax.fori_loop(1, parts, send_scale, 0)
-
     local[4].wait()
     stage(v_rows, v_sent)
-    spread(v_sent, v_got, v_sems, 1)
     stage(q_rows, q_sent)
-    spread(q_sent, q_got, q_sems, 2)
+
+    @pl.when(me != 0)
+    def _():
+        pl.semaphore_wait(late_sem, 1)
+        send_keys(0)
+        send_scale(0)
+
+    @pl.when(me == 2)
+    def _():
+        pl.semaphore_wait(late_partner_sem, 1)
+
+    swap.start()
+    fetch.start()
+    to_group(sender(v_sent, v_got, v_sems, 1))
+    to_group(sender(q_sent, q_got, q_sems, 2))
     k_got[me] = k_sent[me]
     v_got[me] = v_sent[me]
     q_got[me] = q_sent[me]
@@ -174,12 +231,19 @@
 
     swap.wait_recv()
 
-    def await_scale(i, carry):
-        s = source_of(me, i)
-        await_bytes(scale_got.at[s], scale_sems.at[s])
-        return carry
-
-    lax.fori_loop(1, parts, await_scale, 0)
+    def from_group(take):
+        def chip(c):
+            for core in range(2):
+                take(source_of(me, c, core))
+
+        over_chips(parts // 2, chip)
+
+    def await_scale(s):
+        @pl.when(s != me)
+        def _():
+            await_bytes(scale_got.at[s, 0:2], scale_sems.at[s])
+
+    from_group(await_scale)
     flipped = jnp.transpose(scale_got[...].reshape(parts * 8, tok))
     for s in range(parts):
         k_scale[s] = jnp.broadcast_to(flipped[:, 8 * s : 8 * s + 1], (tok, 128))
@@ -190,10 +254,8 @@
     k_gain = chosen[1:2, :]
     cross_gain = chosen[2:3, :] * SCORE_SCALE
 
-    def take_keys(i, carry):
-        s = source_of(me, i)
-
-        @pl.when(i > 0)
+    def take_keys(s):
+        @pl.when(s != me)
         def _():
             await_bytes(k_got.at[s], k_sems.at[s])
 
@@ -202,9 +264,8 @@
             lanes = slice(h * HEAD_DIM, (h + 1) * HEAD_DIM)
             normed = k_got[s, :, lanes].astype(jnp.float32) * scale * k_gain[:, lanes]
             k_normed[h, pl.ds(pl.multiple_of(s * tok, tok), tok), :] = normed.astype(jnp.bfloat16)
-        return carry
-
-    lax.fori_loop(0, parts, take_keys, 0)
+
+    from_group(take_keys)
 
     local[5].wait()
     fetch.wait_recv()
@@ -215,19 +276,16 @@
             cross_keys[h, rows, :] = tables[choice, b * 256 : b * 256 + 128, lanes]
             cross_values[h, rows, :] = tables[choice, b * 256 + 128 : b * 256 + 256, lanes]
 
-    def take_values(i, carry):
-        s = source_of(me, i)
-
-        @pl.when(i > 0)
+    def take_values(s):
+        @pl.when(s != me)
         def _():
             await_bytes(v_got.at[s], v_sems.at[s])
 
         for h in range(2):
             lanes = slice(h * HEAD_DIM, (h + 1) * HEAD_DIM)
             v_wide[h, pl.ds(pl.multiple_of(s * tok, tok), tok), :HEAD_DIM] = v_got[s, :, lanes]
-        return carry
-
-    lax.fori_loop(0, parts, take_values, 0)
+
+    from_group(take_values)
 
     position = lax.broadcasted_iota(jnp.int32, (2 * tok, 128), 1)
     visible = [position < lengths_ref[b] for b in range(2)]
@@ -266,8 +324,8 @@
             shares.append((branch * factor).astype(jnp.bfloat16))
         return jnp.concatenate(shares, axis=1)
 
-    def attend(j, carry):
-        s = (source_of(me, 2 * j) // 2) * 2
+    def attend(c):
+        s = (source_of(me, c, 0) // 2) * 2
         for c in range(2):
 
             @pl.when(s + c != me)
@@ -293,18 +351,16 @@
             @pl.when(d != me)
             def _():
                 pltpu.make_async_remote_copy(
-                    src_ref=out_blocks.at[d], dst_ref=out_got.at[me],
+                    src_ref=out_blocks.at[d], dst_ref=out_ref.at[me],
                     send_sem=send_sems.at[4], recv_sem=out_sem,
                     device_id={"seq": d}, device_id_type=MESH,
                 ).start()
 
             @pl.when(d == me)
             def _():
-                out_got[me] = out_blocks[me]
-
-        return carry
-
-    lax.fori_loop(0, parts // 2, attend, 0)
+                pltpu.make_async_copy(out_blocks.at[me], out_ref.at[me], out_sem).start()
+
+    over_chips(parts // 2, attend)
 
     swap.wait_send()
     fetch.wait_send()
@@ -312,12 +368,27 @@
     await_bytes(k_got.at[some], send_sems.at[0])
     await_bytes(v_got.at[some], send_sems.at[1])
     await_bytes(q_got.at[some], send_sems.at[2])
-    await_bytes(scale_got.at[some], send_sems.at[3])
+    await_bytes(scale_got.at[some, 0:2], send_sems.at[3])
     await_bytes(out_blocks.at[some], send_sems.at[4])
-    await_bytes(out_got.at[some], out_sem)
-
+    await_bytes(out_ref, out_sem)
+
+
+def arrange(steps_ref, got_ref, out_ref, rows, in_sems, out_sems):
+    parts, _, cols = got_ref.shape
+    choice = choice_of(steps_ref)
+    loads, stores = [], []
     for d in range(parts):
-        out_ref[:, d * cols : (d + 1) * cols] = pick(out_got[d], out_got[across(d)])
+        worker = d + choice * (across(d) - d)
+        lanes = slice(d * cols, (d + 1) * cols)
+        loads.append(pltpu.make_async_copy(got_ref.at[worker], rows.at[d], in_sems.at[d]))
+        stores.append(pltpu.make_async_copy(rows.at[d], out_ref.at[:, lanes], out_sems.at[d]))
+    for load in loads:
+        load.start()
+    for load, store in zip(loads, stores):
+        load.wait()
+        store.start()
+    for store in stores:
+        store.wait()
 
 
 def body(q, k, v, timesteps, norm_gain, cross_gain, prompts, lengths):
@@ -330,11 +401,11 @@
     smem = pl.BlockSpec(memory_space=pltpu.SMEM)
     dma = pltpu.SemaphoreType.DMA
     blocks = pltpu.VMEM((parts, tok, cols), bf16)
-    out = pl.pallas_call(
+    got = pl.pallas_call(
         functools.partial(kernel, (parts, tok, cols)),
-        out_shape=jax.ShapeDtypeStruct((tok, width), bf16),
+        out_shape=jax.ShapeDtypeStruct((parts, tok, cols), bf16),
         in_specs=[smem, smem] + [hbm] * 6,
-        out_specs=pl.BlockSpec(memory_space=pltpu.VMEM),
+        out_specs=hbm,
         scratch_shapes=[
             pltpu.VMEM((tok, width), bf16),
             pltpu.VMEM((tok, width), bf16),
@@ -345,7 +416,7 @@
             blocks, blocks, blocks,
             pltpu.VMEM((2, parts * tok, HEAD_DIM), bf16),
             pltpu.VMEM((2, parts * tok, 2 * HEAD_DIM), bf16),
-            blocks, blocks,
+            blocks,
             pltpu.VMEM((8, tok), f32),
             pltpu.VMEM((parts, 8, tok), f32),
             pltpu.VMEM((parts, tok, 128), f32),
@@ -364,6 +435,8 @@
             dma,
             dma,
             dma,
+            pltpu.SemaphoreType.REGULAR,
+            pltpu.SemaphoreType.REGULAR,
         ],
         compiler_params=pltpu.CompilerParams(
             collective_id=0, has_side_effects=True, vmem_limit_bytes=63 * 2**20
@@ -374,6 +447,15 @@
         q.reshape(tok, width), k.reshape(tok, width), v.reshape(tok, width),
         norm_gain.reshape(2, width), cross_gain, prompts.reshape(4 * text, cols),
     )
+    out = pl.pallas_call(
+        arrange,
+        out_shape=jax.ShapeDtypeStruct((tok, width), bf16),
+        in_specs=[smem, hbm],
+        out_specs=hbm,
+        scratch_shapes=[blocks, dma((parts,)), dma((parts,))],
+        compiler_params=pltpu.CompilerParams(vmem_limit_bytes=63 * 2**20),
+        name="arrange",
+    )(timesteps, got)
     return out[None]
 
 

time: 67.1 us -> 60.7 us (0.905)
  Pallas kernels: 64 us -> 59.9 us
  local copies, waits for them, and re-layouts: 2.29 us -> 0 us
    pallas_call x1, Pallas kernels: 64 us -> 57.7 us  [body(): pl.pallas_call(functools.partial(kernel, (parts, tok, cols)), out_shape=j...]
    unnamed x1 -> x0, local copies, waits for them, and re-layouts: 2.29 us -> none
    pallas_call x0 -> x1, Pallas kernels: none -> 2.17 us  [body(): pl.pallas_call(arrange, out_shape=jax.ShapeDtypeStruct((tok, width), bf16...]
where the time goes in v3:
time: 60.7 us; the launch traced here: 60.5 us
  Pallas kernels  59.9 us (99%)
  between operations  0.66 us (1%)
    pallas_call x1, Pallas kernels, body(): pl.pallas_call(functools.partial(kernel, (parts, tok, cols)), out_shape=j...  57.7 us
    pallas_call x1, Pallas kernels, body(): pl.pallas_call(arrange, out_shape=jax.ShapeDtypeStruct((tok, width), bf16...  2.17 us

profile of v3, /device:TPU:1, one launch (start us, length us, event | category | flops | bytes accessed | tf_op | source)
XLA Modules:
  0.0 60.5 jit_solution(6910646309799128417)
XLA Ops:
  0.7 57.7 %guided_attention.1.got_ref = bf16[16,128,256]{2,1,0:T(8,128)(2,1)} custom-call(s32[1]{0:T(128)S(6)} %copy.9.steps_ref, s32[2]{0:T(128)} %lengths_ref.1, bf16[128,4096]{1,0:T(8,128)(2,1)} %bitcast.6, bf16[128,4096]{1,0:T(8,128)(2,1)} %bitcast.7, bf16[128,4096]{1,0:T(8,128)(2,1)} %bitcast.8, bf16[2,4096]{1,0:T(2,128)(2,1)} %bitcast.10, ...), custom_call_target="tpu_custom_call" | custom-call | tf_op jit(solution)/shard_map/guided_attention/pallas_call | solution.py:404
  58.4 2.2 %arrange.1 = bf16[128,4096]{1,0:T(8,128)(2,1)} custom-call(s32[1]{0:T(128)S(6)} %copy.9.steps_ref, bf16[16,128,256]{2,1,0:T(8,128)(2,1)} %guided_attention.1.got_ref), custom_call_target="tpu_custom_call" | custom-call | tf_op jit(solution)/shard_map/arrange/pallas_call | solution.py:450

commit v4 on v3

--- a/solution.py
+++ b/solution.py
@@ -22,12 +22,12 @@
 CHIP_CODE = sum(chip * 8**i for i, chip in enumerate(CHIPS))
 
 
-def over_chips(count, visit):
+def over_chips(count, visit, at_once=1):
     def step(_, code):
-        visit(code % 8)
-        return code // 8
-
-    lax.fori_loop(0, count, step, jnp.int32(CHIP_CODE))
+        visit(*(code // 8**i % 8 for i in range(at_once)))
+        return code // 8**at_once
+
+    lax.fori_loop(0, count // at_once, step, jnp.int32(CHIP_CODE))
 
 
 def shifted(me, y_steps, x_steps, core_steps):
@@ -55,9 +55,9 @@
 
 def kernel(
     sizes,
-    steps_ref, lengths_ref, q_ref, k_ref, v_ref, gain_ref, cross_gain_ref, prompt_ref,
+    steps_ref, length_ref, q_ref, k_ref, v_ref, gain_ref, cross_gain_ref, prompt_ref,
     out_ref,
-    q_rows, k_rows, v_rows, gain_rows, cross_rows,
+    lengths_ref, q_rows, k_rows, v_rows, gain_rows, cross_rows,
     q_sent, k_sent, v_sent,
     q_got, k_got, v_got,
     k_normed, v_wide, out_blocks,
@@ -101,6 +101,7 @@
         pltpu.make_async_copy(q_ref, q_rows, row_sems.at[3]),
         pltpu.make_async_copy(v_ref, v_rows, row_sems.at[4]),
         pltpu.make_async_copy(prompt_ref, tables.at[0], table_own_sem),
+        pltpu.make_async_copy(length_ref, lengths_ref, row_sems.at[5]),
     ]
     for copy in local:
         copy.start()
@@ -268,6 +269,7 @@
     from_group(take_keys)
 
     local[5].wait()
+    local[6].wait()
     fetch.wait_recv()
     for h in range(2):
         lanes = slice(h * HEAD_DIM, (h + 1) * HEAD_DIM)
@@ -287,15 +289,21 @@
 
     from_group(take_values)
 
-    position = lax.broadcasted_iota(jnp.int32, (2 * tok, 128), 1)
+    position = lax.broadcasted_iota(jnp.int32, (4 * tok, 128), 1)
     visible = [position < lengths_ref[b] for b in range(2)]
     weight = (GUIDANCE, 1.0 - GUIDANCE)
 
-    def self_scores(pair, h):
+    def self_scores(blocks, h):
         lanes = slice(h * HEAD_DIM, (h + 1) * HEAD_DIM)
-        rows = q_got[pair, :, lanes].reshape(2 * tok, HEAD_DIM).astype(jnp.float32)
-        scale = q_scale[pair].reshape(2 * tok, 128)
-        query = (rows * scale * q_gain[:, lanes]).astype(jnp.bfloat16)
+        query = jnp.concatenate(
+            [
+                (q_got[d, :, lanes].astype(jnp.float32) * q_scale[d] * q_gain[:, lanes]).astype(
+                    jnp.bfloat16
+                )
+                for d in blocks
+            ],
+            axis=0,
+        )
         return lax.dot_general(query, k_normed[h], NT, preferred_element_type=jnp.float32)
 
     def softmax_weights(scores):
@@ -324,17 +332,19 @@
             shares.append((branch * factor).astype(jnp.bfloat16))
         return jnp.concatenate(shares, axis=1)
 
-    def attend(c):
-        s = (source_of(me, c, 0) // 2) * 2
-        for c in range(2):
-
-            @pl.when(s + c != me)
+    def attend(*chips):
+        blocks = []
+        for c in chips:
+            first = (source_of(me, c, 0) // 2) * 2
+            blocks += [first, first + 1]
+        for d in blocks:
+
+            @pl.when(d != me)
             def _():
-                await_bytes(q_got.at[s + c], q_sems.at[s + c])
-
-        pair = pl.ds(s, 2)
+                await_bytes(q_got.at[d], q_sems.at[d])
+
         heads = range(2)
-        scores = [self_scores(pair, h) for h in heads]
+        scores = [self_scores(blocks, h) for h in heads]
         weights = [softmax_weights(scores[h]) for h in heads]
         self_out = [self_values(weights[h], h) for h in heads]
         scores = [cross_scores(self_out[h], h) for h in heads]
@@ -344,9 +354,10 @@
             guided = self_out[h] + jnp.dot(
                 shares[h], cross_values[h], preferred_element_type=jnp.float32
             )
-            out_blocks[pair, :, lanes] = guided.astype(jnp.bfloat16).reshape(2, tok, HEAD_DIM)
-        for c in range(2):
-            d = s + c
+            guided = guided.astype(jnp.bfloat16)
+            for i, d in enumerate(blocks):
+                out_blocks[d, :, lanes] = guided[i * tok : (i + 1) * tok]
+        for d in blocks:
 
             @pl.when(d != me)
             def _():
@@ -360,7 +371,7 @@
             def _():
                 pltpu.make_async_copy(out_blocks.at[me], out_ref.at[me], out_sem).start()
 
-    over_chips(parts // 2, attend)
+    over_chips(parts // 2, attend, at_once=2)
 
     swap.wait_send()
     fetch.wait_send()
@@ -373,22 +384,18 @@
     await_bytes(out_ref, out_sem)
 
 
-def arrange(steps_ref, got_ref, out_ref, rows, in_sems, out_sems):
+def arrange(steps_ref, got_ref, out_ref, sems):
     parts, _, cols = got_ref.shape
     choice = choice_of(steps_ref)
-    loads, stores = [], []
+    copies = []
     for d in range(parts):
         worker = d + choice * (across(d) - d)
         lanes = slice(d * cols, (d + 1) * cols)
-        loads.append(pltpu.make_async_copy(got_ref.at[worker], rows.at[d], in_sems.at[d]))
-        stores.append(pltpu.make_async_copy(rows.at[d], out_ref.at[:, lanes], out_sems.at[d]))
-    for load in loads:
-        load.start()
-    for load, store in zip(loads, stores):
-        load.wait()
-        store.start()
-    for store in stores:
-        store.wait()
+        copies.append(pltpu.make_async_copy(got_ref.at[worker], out_ref.at[:, lanes], sems.at[d]))
+    for copy in copies:
+        copy.start()
+    for copy in copies:
+        copy.wait()
 
 
 def body(q, k, v, timesteps, norm_gain, cross_gain, prompts, lengths):
@@ -398,15 +405,17 @@
     text = prompts.shape[3]
     bf16, f32 = jnp.bfloat16, jnp.float32
     hbm = pl.BlockSpec(memory_space=pltpu.HBM)
+    vmem = pl.BlockSpec(memory_space=pltpu.VMEM)
     smem = pl.BlockSpec(memory_space=pltpu.SMEM)
     dma = pltpu.SemaphoreType.DMA
     blocks = pltpu.VMEM((parts, tok, cols), bf16)
     got = pl.pallas_call(
         functools.partial(kernel, (parts, tok, cols)),
-        out_shape=jax.ShapeDtypeStruct((parts, tok, cols), bf16),
-        in_specs=[smem, smem] + [hbm] * 6,
-        out_specs=hbm,
+        out_shape=blocks,
+        in_specs=[smem] + [hbm] * 7,
+        out_specs=vmem,
         scratch_shapes=[
+            pltpu.SMEM((2,), jnp.int32),
             pltpu.VMEM((tok, width), bf16),
             pltpu.VMEM((tok, width), bf16),
             pltpu.VMEM((tok, width), bf16),
@@ -425,7 +434,7 @@
             pltpu.VMEM((2, 4 * text, cols), bf16),
             pltpu.VMEM((2, 2 * text, HEAD_DIM), bf16),
             pltpu.VMEM((2, 2 * text, HEAD_DIM), bf16),
-            dma((5,)),
+            dma((6,)),
             dma((parts,)),
             dma((parts,)),
             dma((parts,)),
@@ -439,21 +448,27 @@
             pltpu.SemaphoreType.REGULAR,
         ],
         compiler_params=pltpu.CompilerParams(
-            collective_id=0, has_side_effects=True, vmem_limit_bytes=63 * 2**20
+            collective_id=0, has_side_effects=True, vmem_limit_bytes=44 * 2**20
         ),
         name="guided_attention",
     )(
-        timesteps, lengths,
-        q.reshape(tok, width), k.reshape(tok, width), v.reshape(tok, width),
-        norm_gain.reshape(2, width), cross_gain, prompts.reshape(4 * text, cols),
+        timesteps,
+        *(
+            pltpu.with_memory_space_constraint(x, pltpu.HBM)
+            for x in (
+                lengths,
+                q.reshape(tok, width), k.reshape(tok, width), v.reshape(tok, width),
+                norm_gain.reshape(2, width), cross_gain, prompts.reshape(4 * text, cols),
+            )
+        ),
     )
     out = pl.pallas_call(
         arrange,
         out_shape=jax.ShapeDtypeStruct((tok, width), bf16),
-        in_specs=[smem, hbm],
+        in_specs=[smem, vmem],
         out_specs=hbm,
-        scratch_shapes=[blocks, dma((parts,)), dma((parts,))],
-        compiler_params=pltpu.CompilerParams(vmem_limit_bytes=63 * 2**20),
+        scratch_shapes=[dma((parts,))],
+        compiler_params=pltpu.CompilerParams(vmem_limit_bytes=8 * 2**20),
         name="arrange",
     )(timesteps, got)
     return out[None]

time: 60.7 us -> 60.2 us (level)
    pallas_call x1, Pallas kernels: 2.17 us -> 1.1 us  [body(): pl.pallas_call(arrange, out_shape=jax.ShapeDtypeStruct((tok, width), bf16...]
    pallas_call x1, Pallas kernels: 57.7 us -> 58.3 us  [body(): pl.pallas_call(functools.partial(kernel, (parts, tok, cols)), out_shape=b...]
where the time goes in v4:
time: 60.2 us; the launch traced here: 60.1 us
  Pallas kernels  59.5 us (99%)
  between operations  0.66 us (1%)
    pallas_call x1, Pallas kernels, body(): pl.pallas_call(functools.partial(kernel, (parts, tok, cols)), out_shape=b...  58.3 us

profile of v4, /device:TPU:1, one launch (start us, length us, event | category | flops | bytes accessed | tf_op | source)
XLA Modules:
  0.0 60.1 jit_solution(6560822796778490297)
XLA Ops:
  0.7 58.3 %guided_attention.1.got_ref = bf16[16,128,256]{2,1,0:T(8,128)(2,1)S(1)} custom-call(s32[1]{0:T(128)S(6)} %copy.9.steps_ref, s32[2]{0:T(128)} %length_ref.1, bf16[128,4096]{1,0:T(8,128)(2,1)} %bitcast.6, bf16[128,4096]{1,0:T(8,128)(2,1)} %bitcast.7, bf16[128,4096]{1,0:T(8,128)(2,1)} %bitcast.8, bf16[2,4096]{1,0:T(2,128)(2,1)} %bitcast.10, ...), custom_call_target="tpu_custom_call" | custom-call | tf_op jit(solution)/shard_map/guided_attention/pallas_call | solution.py:412
  59.0 1.1 %arrange.1 = bf16[128,4096]{1,0:T(8,128)(2,1)} custom-call(s32[1]{0:T(128)S(6)} %copy.9.steps_ref, bf16[16,128,256]{2,1,0:T(8,128)(2,1)S(1)} %guided_attention.1.got_ref), custom_call_target="tpu_custom_call" | custom-call | tf_op jit(solution)/shard_map/arrange/pallas_call | solution.py:465

commit v5 on v4

--- a/solution.py
+++ b/solution.py
@@ -110,7 +110,9 @@
         def one(d, carry):
             here = pl.ds(pl.multiple_of(d * cols, cols), cols)
             there = pl.ds(pl.multiple_of(across(d) * cols, cols), cols)
-            sent[d] = pick(rows[:, here], rows[:, there])
+            both = pick(rows[:, here], rows[:, there])
+            for h in range(2):
+                sent[h, d] = both[:, h * HEAD_DIM : (h + 1) * HEAD_DIM]
             return carry
 
         lax.fori_loop(0, parts, one, 0)
@@ -123,11 +125,11 @@
         over_chips(parts // 2 - 1, chip)
         send(shifted(me, 0, 0, 1))
 
-    def sender(sent, got, sems, kind):
+    def sender(sent, got, sems, kind, h):
         def send(d):
             pltpu.make_async_remote_copy(
-                src_ref=sent.at[d], dst_ref=got.at[me],
-                send_sem=send_sems.at[kind], recv_sem=sems.at[me],
+                src_ref=sent.at[h, d], dst_ref=got.at[h, me],
+                send_sem=send_sems.at[2 * kind + h], recv_sem=sems.at[h, me],
                 device_id={"seq": d}, device_id_type=MESH,
             ).start()
 
@@ -136,7 +138,7 @@
     def send_scale(d):
         pltpu.make_async_remote_copy(
             src_ref=scale_own.at[0:2], dst_ref=scale_got.at[me, 0:2],
-            send_sem=send_sems.at[3], recv_sem=scale_sems.at[me],
+            send_sem=send_sems.at[8], recv_sem=scale_sems.at[me],
             device_id={"seq": d}, device_id_type=MESH,
         ).start()
 
@@ -168,7 +170,7 @@
     def _():
         pl.semaphore_wait(barrier, parts - 1)
 
-    send_keys = sender(k_sent, k_got, k_sems, 0)
+    send_keys = sender(k_sent, k_got, k_sems, 0, 0)
     to_group(but_first(send_keys))
 
     def inverse_rms(rows):
@@ -199,16 +201,25 @@
     gains[0, 3:8, :] = jnp.zeros((5, cols), jnp.float32)
     swap = pltpu.make_async_remote_copy(
         src_ref=gains.at[0], dst_ref=gains.at[1],
-        send_sem=send_sems.at[6], recv_sem=gain_sem,
+        send_sem=send_sems.at[9], recv_sem=gain_sem,
         device_id=partner, device_id_type=MESH,
     )
     fetch = pltpu.make_async_remote_copy(
         src_ref=prompt_ref, dst_ref=tables.at[1],
-        send_sem=send_sems.at[5], recv_sem=table_sem,
+        send_sem=send_sems.at[10], recv_sem=table_sem,
         device_id=partner, device_id_type=MESH,
     )
+
+    @pl.when(me == 2)
+    def _():
+        pl.semaphore_wait(late_partner_sem, 1)
+
+    swap.start()
+    fetch.start()
     local[4].wait()
     stage(v_rows, v_sent)
+    send_values = sender(v_sent, v_got, v_sems, 1, 0)
+    to_group(but_first(send_values))
     stage(q_rows, q_sent)
 
     @pl.when(me != 0)
@@ -216,18 +227,16 @@
         pl.semaphore_wait(late_sem, 1)
         send_keys(0)
         send_scale(0)
-
-    @pl.when(me == 2)
-    def _():
-        pl.semaphore_wait(late_partner_sem, 1)
-
-    swap.start()
-    fetch.start()
-    to_group(sender(v_sent, v_got, v_sems, 1))
-    to_group(sender(q_sent, q_got, q_sems, 2))
-    k_got[me] = k_sent[me]
-    v_got[me] = v_sent[me]
-    q_got[me] = q_sent[me]
+        send_values(0)
+
+    to_group(sender(q_sent, q_got, q_sems, 2, 0))
+    to_group(sender(k_sent, k_got, k_sems, 0, 1))
+    to_group(sender(v_sent, v_got, v_sems, 1, 1))
+    to_group(sender(q_sent, q_got, q_sems, 2, 1))
+    for h in range(2):
+        k_got[h, me] = k_sent[h, me]
+        v_got[h, me] = v_sent[h, me]
+        q_got[h, me] = q_sent[h, me]
     v_wide[:, :, HEAD_DIM:] = jnp.ones((2, parts * tok, HEAD_DIM), jnp.bfloat16)
 
     swap.wait_recv()
@@ -255,18 +264,27 @@
     k_gain = chosen[1:2, :]
     cross_gain = chosen[2:3, :] * SCORE_SCALE
 
-    def take_keys(s):
+    def take_keys(s, h):
         @pl.when(s != me)
         def _():
-            await_bytes(k_got.at[s], k_sems.at[s])
-
-        scale = k_scale[s]
-        for h in range(2):
-            lanes = slice(h * HEAD_DIM, (h + 1) * HEAD_DIM)
-            normed = k_got[s, :, lanes].astype(jnp.float32) * scale * k_gain[:, lanes]
-            k_normed[h, pl.ds(pl.multiple_of(s * tok, tok), tok), :] = normed.astype(jnp.bfloat16)
-
-    from_group(take_keys)
+            await_bytes(k_got.at[h, s], k_sems.at[h, s])
+
+        lanes = slice(h * HEAD_DIM, (h + 1) * HEAD_DIM)
+        normed = k_got[h, s].astype(jnp.float32) * k_scale[s] * k_gain[:, lanes]
+        k_normed[h, pl.ds(pl.multiple_of(s * tok, tok), tok), :] = normed.astype(jnp.bfloat16)
+
+    def take_values(s, h):
+        @pl.when(s != me)
+        def _():
+            await_bytes(v_got.at[h, s], v_sems.at[h, s])
+
+        v_wide[h, pl.ds(pl.multiple_of(s * tok, tok), tok), :HEAD_DIM] = v_got[h, s]
+
+    def take(h):
+        from_group(lambda s: take_keys(s, h))
+        from_group(lambda s: take_values(s, h))
+
+    take(0)
 
     local[5].wait()
     local[6].wait()
@@ -278,17 +296,6 @@
             cross_keys[h, rows, :] = tables[choice, b * 256 : b * 256 + 128, lanes]
             cross_values[h, rows, :] = tables[choice, b * 256 + 128 : b * 256 + 256, lanes]
 
-    def take_values(s):
-        @pl.when(s != me)
-        def _():
-            await_bytes(v_got.at[s], v_sems.at[s])
-
-        for h in range(2):
-            lanes = slice(h * HEAD_DIM, (h + 1) * HEAD_DIM)
-            v_wide[h, pl.ds(pl.multiple_of(s * tok, tok), tok), :HEAD_DIM] = v_got[s, :, lanes]
-
-    from_group(take_values)
-
     position = lax.broadcasted_iota(jnp.int32, (4 * tok, 128), 1)
     visible = [position < lengths_ref[b] for b in range(2)]
     weight = (GUIDANCE, 1.0 - GUIDANCE)
@@ -297,7 +304,7 @@
         lanes = slice(h * HEAD_DIM, (h + 1) * HEAD_DIM)
         query = jnp.concatenate(
             [
-                (q_got[d, :, lanes].astype(jnp.float32) * q_scale[d] * q_gain[:, lanes]).astype(
+                (q_got[h, d].astype(jnp.float32) * q_scale[d] * q_gain[:, lanes]).astype(
                     jnp.bfloat16
                 )
                 for d in blocks
@@ -332,7 +339,7 @@
             shares.append((branch * factor).astype(jnp.bfloat16))
         return jnp.concatenate(shares, axis=1)
 
-    def attend(*chips):
+    def attend(h, *chips):
         blocks = []
         for c in chips:
             first = (source_of(me, c, 0) // 2) * 2
@@ -341,46 +348,52 @@
 
             @pl.when(d != me)
             def _():
-                await_bytes(q_got.at[d], q_sems.at[d])
-
-        heads = range(2)
-        scores = [self_scores(blocks, h) for h in heads]
-        weights = [softmax_weights(scores[h]) for h in heads]
-        self_out = [self_values(weights[h], h) for h in heads]
-        scores = [cross_scores(self_out[h], h) for h in heads]
-        shares = [cross_weights(scores[h]) for h in heads]
-        for h in heads:
-            lanes = slice(h * HEAD_DIM, (h + 1) * HEAD_DIM)
-            guided = self_out[h] + jnp.dot(
-                shares[h], cross_values[h], preferred_element_type=jnp.float32
+                await_bytes(q_got.at[h, d], q_sems.at[h, d])
+
+        halves = [blocks[:4], blocks[4:]]
+        scores = [self_scores(half, h) for half in halves]
+        weights = [softmax_weights(x) for x in scores]
+        self_out = [self_values(x, h) for x in weights]
+        scores = [cross_scores(x, h) for x in self_out]
+        shares = [cross_weights(x) for x in scores]
+        for i, half in enumerate(halves):
+            guided = self_out[i] + jnp.dot(
+                shares[i], cross_values[h], preferred_element_type=jnp.float32
             )
             guided = guided.astype(jnp.bfloat16)
-            for i, d in enumerate(blocks):
-                out_blocks[d, :, lanes] = guided[i * tok : (i + 1) * tok]
+            for j, d in enumerate(half):
+                out_blocks[h, d] = guided[j * tok : (j + 1) * tok]
+        lanes = pl.ds(h * HEAD_DIM, HEAD_DIM)
         for d in blocks:
 
             @pl.when(d != me)
             def _():
                 pltpu.make_async_remote_copy(
-                    src_ref=out_blocks.at[d], dst_ref=out_ref.at[me],
-                    send_sem=send_sems.at[4], recv_sem=out_sem,
+                    src_ref=out_blocks.at[h, d], dst_ref=out_ref.at[me, :, lanes],
+                    send_sem=send_sems.at[6 + h], recv_sem=out_sem,
                     device_id={"seq": d}, device_id_type=MESH,
                 ).start()
 
             @pl.when(d == me)
             def _():
-                pltpu.make_async_copy(out_blocks.at[me], out_ref.at[me], out_sem).start()
-
-    over_chips(parts // 2, attend, at_once=2)
+                pltpu.make_async_copy(
+                    out_blocks.at[h, me], out_ref.at[me, :, lanes], out_sem
+                ).start()
+
+    for h in range(2):
+        if h == 1:
+            take(1)
+        over_chips(parts // 2, functools.partial(attend, h), at_once=4)
 
     swap.wait_send()
     fetch.wait_send()
     some = pl.ds(0, parts - 1)
-    await_bytes(k_got.at[some], send_sems.at[0])
-    await_bytes(v_got.at[some], send_sems.at[1])
-    await_bytes(q_got.at[some], send_sems.at[2])
-    await_bytes(scale_got.at[some, 0:2], send_sems.at[3])
-    await_bytes(out_blocks.at[some], send_sems.at[4])
+    for h in range(2):
+        await_bytes(k_got.at[h, some], send_sems.at[h])
+        await_bytes(v_got.at[h, some], send_sems.at[2 + h])
+        await_bytes(q_got.at[h, some], send_sems.at[4 + h])
+        await_bytes(out_blocks.at[h, some], send_sems.at[6 + h])
+    await_bytes(scale_got.at[some, 0:2], send_sems.at[8])
     await_bytes(out_ref, out_sem)
 
 
@@ -408,10 +421,10 @@
     vmem = pl.BlockSpec(memory_space=pltpu.VMEM)
     smem = pl.BlockSpec(memory_space=pltpu.SMEM)
     dma = pltpu.SemaphoreType.DMA
-    blocks = pltpu.VMEM((parts, tok, cols), bf16)
+    blocks = pltpu.VMEM((2, parts, tok, HEAD_DIM), bf16)
     got = pl.pallas_call(
         functools.partial(kernel, (parts, tok, cols)),
-        out_shape=blocks,
+        out_shape=pltpu.VMEM((parts, tok, cols), bf16),
         in_specs=[smem] + [hbm] * 7,
         out_specs=vmem,
         scratch_shapes=[
@@ -435,11 +448,11 @@
             pltpu.VMEM((2, 2 * text, HEAD_DIM), bf16),
             pltpu.VMEM((2, 2 * text, HEAD_DIM), bf16),
             dma((6,)),
+            dma((2, parts)),
+            dma((2, parts)),
+            dma((2, parts)),
             dma((parts,)),
-            dma((parts,)),
-            dma((parts,)),
-            dma((parts,)),
-            dma((7,)),
+            dma((11,)),
             dma,
             dma,
             dma,

time: 60.2 us -> 58.8 us (0.977)
  Pallas kernels: 59.5 us -> 58 us
    pallas_call x1, Pallas kernels: 58.3 us -> 56.9 us  [body(): pl.pallas_call(functools.partial(kernel, (parts, tok, cols)), out_shape=p...]
where the time goes in v5:
time: 58.8 us; the launch traced here: 58.7 us
  Pallas kernels  58 us (99%)
  between operations  0.66 us (1%)
    pallas_call x1, Pallas kernels, body(): pl.pallas_call(functools.partial(kernel, (parts, tok, cols)), out_shape=p...  56.9 us

profile of v5, /device:TPU:1, one launch (start us, length us, event | category | flops | bytes accessed | tf_op | source)
XLA Modules:
  0.0 58.7 jit_solution(5857865841365415093)
XLA Ops:
  0.7 56.9 %guided_attention.1.got_ref = bf16[16,128,256]{2,1,0:T(8,128)(2,1)S(1)} custom-call(s32[1]{0:T(128)S(6)} %copy.9.steps_ref, s32[2]{0:T(128)} %length_ref.1, bf16[128,4096]{1,0:T(8,128)(2,1)} %bitcast.6, bf16[128,4096]{1,0:T(8,128)(2,1)} %bitcast.7, bf16[128,4096]{1,0:T(8,128)(2,1)} %bitcast.8, bf16[2,4096]{1,0:T(2,128)(2,1)} %bitcast.10, ...), custom_call_target="tpu_custom_call" | custom-call | tf_op jit(solution)/shard_map/guided_attention/pallas_call | solution.py:425
  57.6 1.1 %arrange.1 = bf16[128,4096]{1,0:T(8,128)(2,1)} custom-call(s32[1]{0:T(128)S(6)} %copy.9.steps_ref, bf16[16,128,256]{2,1,0:T(8,128)(2,1)S(1)} %guided_attention.1.got_ref), custom_call_target="tpu_custom_call" | custom-call | tf_op jit(solution)/shard_map/arrange/pallas_call | solution.py:478

commit v6 on v5

--- a/solution.py
+++ b/solution.py
@@ -77,22 +77,6 @@
 
     partner = {"expert": 1 - expert, "seq": across(me)}
 
-    barrier = pltpu.get_barrier_semaphore()
-
-    def signal_group(sem):
-        def one(i, carry):
-            pl.semaphore_signal(sem, 1, device_id={"seq": (me + i) % parts}, device_id_type=MESH)
-            return carry
-
-        lax.fori_loop(1, parts, one, 0)
-
-    scale_got[...] = jnp.zeros_like(scale_got)
-
-    @pl.when(me != 0)
-    def _():
-        signal_group(barrier)
-        pl.semaphore_signal(barrier, 1, device_id=partner, device_id_type=MESH)
-
     own_cols = pl.ds(pl.multiple_of(me * cols, cols), cols)
     local = [
         pltpu.make_async_copy(k_ref, k_rows, row_sems.at[0]),
@@ -103,7 +87,25 @@
         pltpu.make_async_copy(prompt_ref, tables.at[0], table_own_sem),
         pltpu.make_async_copy(length_ref, lengths_ref, row_sems.at[5]),
     ]
-    for copy in local:
+    local[0].start()
+
+    barrier = pltpu.get_barrier_semaphore()
+
+    def signal_group(sem):
+        def one(i, carry):
+            pl.semaphore_signal(sem, 1, device_id={"seq": (me + i) % parts}, device_id_type=MESH)
+            return carry
+
+        lax.fori_loop(1, parts, one, 0)
+
+    scale_got[...] = jnp.zeros_like(scale_got)
+
+    @pl.when(me != 0)
+    def _():
+        signal_group(barrier)
+        pl.semaphore_signal(barrier, 1, device_id=partner, device_id_type=MESH)
+
+    for copy in local[1:]:
         copy.start()
 
     def stage(rows, sent):
@@ -339,11 +341,23 @@
             shares.append((branch * factor).astype(jnp.bfloat16))
         return jnp.concatenate(shares, axis=1)
 
+    late_chip = ((ROWS_OF_Y - me // 4) % ROWS_OF_Y) * 2 + (me // 2) % 2
+    early = functools.reduce(
+        jnp.logical_or, [late_chip == c for c in CHIPS[: len(CHIPS) // 2]]
+    )
+    stand_in = (source_of(me, CHIPS[len(CHIPS) // 2], 0) // 2) * 2
+
+    def put_off(d):
+        swapped = jnp.where(d == 0, stand_in, jnp.where(d == stand_in, 0, d))
+        return jnp.where(early, swapped, d)
+
     def attend(h, *chips):
         blocks = []
         for c in chips:
             first = (source_of(me, c, 0) // 2) * 2
             blocks += [first, first + 1]
+        if h == 1:
+            blocks = [put_off(d) for d in blocks]
         for d in blocks:
 
             @pl.when(d != me)

time: 58.8 us -> 58.1 us (0.988)
  Pallas kernels: 58 us -> 57.4 us
    pallas_call x1, Pallas kernels: 56.9 us -> 56.3 us  [body(): pl.pallas_call(functools.partial(kernel, (parts, tok, cols)), out_shape=p...]
where the time goes in v6:
time: 58.1 us; the launch traced here: 58 us
  Pallas kernels  57.4 us (99%)
  between operations  0.66 us (1%)
    pallas_call x1, Pallas kernels, body(): pl.pallas_call(functools.partial(kernel, (parts, tok, cols)), out_shape=p...  56.3 us

profile of v6, /device:TPU:1, one launch (start us, length us, event | category | flops | bytes accessed | tf_op | source)
XLA Modules:
  0.0 58.0 jit_solution(9209079894578564538)
XLA Ops:
  0.7 56.3 %guided_attention.1.got_ref = bf16[16,128,256]{2,1,0:T(8,128)(2,1)S(1)} custom-call(s32[1]{0:T(128)S(6)} %copy.9.steps_ref, s32[2]{0:T(128)} %length_ref.1, bf16[128,4096]{1,0:T(8,128)(2,1)} %bitcast.6, bf16[128,4096]{1,0:T(8,128)(2,1)} %bitcast.7, bf16[128,4096]{1,0:T(8,128)(2,1)} %bitcast.8, bf16[2,4096]{1,0:T(2,128)(2,1)} %bitcast.10, ...), custom_call_target="tpu_custom_call" | custom-call | tf_op jit(solution)/shard_map/guided_attention/pallas_call | solution.py:439
  56.9 1.1 %arrange.1 = bf16[128,4096]{1,0:T(8,128)(2,1)} custom-call(s32[1]{0:T(128)S(6)} %copy.9.steps_ref, bf16[16,128,256]{2,1,0:T(8,128)(2,1)S(1)} %guided_attention.1.got_ref), custom_call_target="tpu_custom_call" | custom-call | tf_op jit(solution)/shard_map/arrange/pallas_call | solution.py:492

commit v7 on v6

--- a/solution.py
+++ b/solution.py
@@ -342,14 +342,19 @@
         return jnp.concatenate(shares, axis=1)
 
     late_chip = ((ROWS_OF_Y - me // 4) % ROWS_OF_Y) * 2 + (me // 2) % 2
-    early = functools.reduce(
-        jnp.logical_or, [late_chip == c for c in CHIPS[: len(CHIPS) // 2]]
+    half = len(CHIPS) // 2
+    far = late_chip == CHIPS[half - 1]
+    near = functools.reduce(jnp.logical_or, [late_chip == c for c in CHIPS[half:-1]])
+    give = jnp.where(far, 0, 1)
+    take_up = jnp.where(
+        far,
+        (source_of(me, CHIPS[half], 0) // 2) * 2,
+        (source_of(me, CHIPS[half - 1], 0) // 2) * 2 + 1,
     )
-    stand_in = (source_of(me, CHIPS[len(CHIPS) // 2], 0) // 2) * 2
 
     def put_off(d):
-        swapped = jnp.where(d == 0, stand_in, jnp.where(d == stand_in, 0, d))
-        return jnp.where(early, swapped, d)
+        swapped = jnp.where(d == give, take_up, jnp.where(d == take_up, give, d))
+        return jnp.where(far | near, swapped, d)
 
     def attend(h, *chips):
         blocks = []
@@ -378,15 +383,25 @@
             for j, d in enumerate(half):
                 out_blocks[h, d] = guided[j * tok : (j + 1) * tok]
         lanes = pl.ds(h * HEAD_DIM, HEAD_DIM)
+
+        def send_out(d):
+            pltpu.make_async_remote_copy(
+                src_ref=out_blocks.at[h, d], dst_ref=out_ref.at[me, :, lanes],
+                send_sem=send_sems.at[6 + h], recv_sem=out_sem,
+                device_id={"seq": d}, device_id_type=MESH,
+            ).start()
+
+        holds_first = functools.reduce(jnp.logical_or, [d == 0 for d in blocks])
+
+        @pl.when(holds_first & (me != 0))
+        def _():
+            send_out(0)
+
         for d in blocks:
 
-            @pl.when(d != me)
+            @pl.when((d != me) & (d != 0))
             def _():
-                pltpu.make_async_remote_copy(
-                    src_ref=out_blocks.at[h, d], dst_ref=out_ref.at[me, :, lanes],
-                    send_sem=send_sems.at[6 + h], recv_sem=out_sem,
-                    device_id={"seq": d}, device_id_type=MESH,
-                ).start()
+                send_out(d)
 
             @pl.when(d == me)
             def _():

time: 58.1 us -> 57.6 us (level)
  Pallas kernels: 57.4 us -> 56.8 us
where the time goes in v7:
time: 57.6 us; the launch traced here: 57.5 us
  Pallas kernels  56.8 us (99%)
  between operations  0.66 us (1%)
    pallas_call x1, Pallas kernels, body(): pl.pallas_call(functools.partial(kernel, (parts, tok, cols)), out_shape=p...  55.7 us

profile of v7, /device:TPU:1, one launch (start us, length us, event | category | flops | bytes accessed | tf_op | source)
XLA Modules:
  0.0 57.5 jit_solution(14639772263833865634)
XLA Ops:
  0.7 55.7 %guided_attention.1.got_ref = bf16[16,128,256]{2,1,0:T(8,128)(2,1)S(1)} custom-call(s32[1]{0:T(128)S(6)} %copy.9.steps_ref, s32[2]{0:T(128)} %length_ref.1, bf16[128,4096]{1,0:T(8,128)(2,1)} %bitcast.6, bf16[128,4096]{1,0:T(8,128)(2,1)} %bitcast.7, bf16[128,4096]{1,0:T(8,128)(2,1)} %bitcast.8, bf16[2,4096]{1,0:T(2,128)(2,1)} %bitcast.10, ...), custom_call_target="tpu_custom_call" | custom-call | tf_op jit(solution)/shard_map/guided_attention/pallas_call | solution.py:454
  56.4 1.1 %arrange.1 = bf16[128,4096]{1,0:T(8,128)(2,1)} custom-call(s32[1]{0:T(128)S(6)} %copy.9.steps_ref, bf16[16,128,256]{2,1,0:T(8,128)(2,1)S(1)} %guided_attention.1.got_ref), custom_call_target="tpu_custom_call" | custom-call | tf_op jit(solution)/shard_map/arrange/pallas_call | solution.py:507

commit v8 on v7

--- a/solution.py
+++ b/solution.py
@@ -108,13 +108,12 @@
     for copy in local[1:]:
         copy.start()
 
-    def stage(rows, sent):
+    def stage(rows, sent, heads):
         def one(d, carry):
-            here = pl.ds(pl.multiple_of(d * cols, cols), cols)
-            there = pl.ds(pl.multiple_of(across(d) * cols, cols), cols)
-            both = pick(rows[:, here], rows[:, there])
-            for h in range(2):
-                sent[h, d] = both[:, h * HEAD_DIM : (h + 1) * HEAD_DIM]
+            for h in heads:
+                here = pl.multiple_of(d * cols + h * HEAD_DIM, HEAD_DIM)
+                there = pl.multiple_of(across(d) * cols + h * HEAD_DIM, HEAD_DIM)
+                sent[h, d] = pick(rows[:, pl.ds(here, HEAD_DIM)], rows[:, pl.ds(there, HEAD_DIM)])
             return carry
 
         lax.fori_loop(0, parts, one, 0)
@@ -156,24 +155,27 @@
         pltpu.make_async_copy(ref, ref, sem).wait()
 
     local[0].wait()
-    stage(k_rows, k_sent)
+    stage(k_rows, k_sent, (0,))
 
     @pl.when(me == 0)
     def _():
         pl.semaphore_wait(barrier, parts)
+
+    @pl.when(me == 2)
+    def _():
+        pl.semaphore_wait(barrier, parts - 2)
+
+    @pl.when((me != 0) & (me != 2))
+    def _():
+        pl.semaphore_wait(barrier, parts - 1)
+
+    send_keys = sender(k_sent, k_got, k_sems, 0, 0)
+    to_group(but_first(send_keys))
+
+    @pl.when(me == 0)
+    def _():
         signal_group(late_sem)
         pl.semaphore_signal(late_partner_sem, 1, device_id=partner, device_id_type=MESH)
-
-    @pl.when(me == 2)
-    def _():
-        pl.semaphore_wait(barrier, parts - 2)
-
-    @pl.when((me != 0) & (me != 2))
-    def _():
-        pl.semaphore_wait(barrier, parts - 1)
-
-    send_keys = sender(k_sent, k_got, k_sems, 0, 0)
-    to_group(but_first(send_keys))
 
     def inverse_rms(rows):
         def add(c, total):
@@ -219,10 +221,11 @@
     swap.start()
     fetch.start()
     local[4].wait()
-    stage(v_rows, v_sent)
+    stage(v_rows, v_sent, (0, 1))
     send_values = sender(v_sent, v_got, v_sems, 1, 0)
     to_group(but_first(send_values))
-    stage(q_rows, q_sent)
+    stage(q_rows, q_sent, (0, 1))
+    stage(k_rows, k_sent, (1,))
 
     @pl.when(me != 0)
     def _():

time: 57.6 us -> 57.6 us (level)
  no operation moved by 1% of the time
where the time goes in v8:
time: 57.6 us; the launch traced here: 57.4 us
  Pallas kernels  56.8 us (99%)
  between operations  0.66 us (1%)
    pallas_call x1, Pallas kernels, body(): pl.pallas_call(functools.partial(kernel, (parts, tok, cols)), out_shape=p...  55.7 us

profile of v8, /device:TPU:1, one launch (start us, length us, event | category | flops | bytes accessed | tf_op | source)
XLA Modules:
  0.0 57.4 jit_solution(6264061402006660563)
XLA Ops:
  0.7 55.7 %guided_attention.1.got_ref = bf16[16,128,256]{2,1,0:T(8,128)(2,1)S(1)} custom-call(s32[1]{0:T(128)S(6)} %copy.9.steps_ref, s32[2]{0:T(128)} %length_ref.1, bf16[128,4096]{1,0:T(8,128)(2,1)} %bitcast.6, bf16[128,4096]{1,0:T(8,128)(2,1)} %bitcast.7, bf16[128,4096]{1,0:T(8,128)(2,1)} %bitcast.8, bf16[2,4096]{1,0:T(2,128)(2,1)} %bitcast.10, ...), custom_call_target="tpu_custom_call" | custom-call | tf_op jit(solution)/shard_map/guided_attention/pallas_call | solution.py:457
  56.3 1.1 %arrange.1 = bf16[128,4096]{1,0:T(8,128)(2,1)} custom-call(s32[1]{0:T(128)S(6)} %copy.9.steps_ref, bf16[16,128,256]{2,1,0:T(8,128)(2,1)S(1)} %guided_attention.1.got_ref), custom_call_target="tpu_custom_call" | custom-call | tf_op jit(solution)/shard_map/arrange/pallas_call | solution.py:510
